TPU v7x, 128 devices: a whole 4x4x4 slice. The times are simulated.
128 devices in a mesh: chan: 32 (over y, x, core), tm: 4 (over z).
Axes of the slice: x: 4, y: 4, z: 4, core: 2. Of those that a mesh axis runs over, the one named last changes fastest.
Arguments:
- record: bfloat16 [4096, 16384], P('chan', 'tm')
- seg_starts: int32 [64], P('tm'), may hold values from 0 to 15872, as said below
- pair_blocks: int32 [93, 2], replicated, may hold values from 0 to 31, as said below
- pair_owner: int32 [93], replicated, may hold values from 0 to 127, as said below
Outputs:
- correlations: bfloat16 [128, 128, 64, 128], P('tm', 'chan')
Inputs may be any that keep to these rules, and one draw needn't show every extreme that they name: `seg_starts`: each segment starts inside the time block of its own segment group: segment s starts between (s // 16) * 16 * 256 and that plus 16 * 256 - 1; every segment ends by 16384. `pair_blocks`: each row is a pair (first, second) with second - first equal to 0, 1 or 2; every such pair of the 32 blocks appears exactly once. `pair_owner`: slots are distinct. The owner (slot // 4) of a pair block (first, second) is first, or, where second - first = 2, first or first + 1. An owner holds at most 4 pair blocks, and some owner holds 4.
All inputs are finite; a program needn't handle non-finite values.
Results may differ from a plain program's by a relative error of at most 0.015.
Values may be sent and summed in bfloat16 or wider, within the bound.
A program may use at most 128 MiB of HBM per device.

v0:
```python
import math

import jax
import jax.numpy as jnp
from jax import lax
from jax.sharding import PartitionSpec as P

SEG_LEN = 512
F = 256
LOW_BIN = 1
NLAG = 64
SLOTS = 4


LEVEL = 0.5
EPS = 1e-06


def passed_along(block, axis, distance):
    devices = range(lax.axis_size(axis))
    route = [(i - distance, i) for i in devices if i - distance in devices]
    return lax.ppermute(block, axis, route)


def transform_table():
    sample = jnp.arange(SEG_LEN, dtype=jnp.int32)
    bins = jnp.arange(F, dtype=jnp.int32) + LOW_BIN
    phase = (bins[:, None] * sample[None, :] % SEG_LEN).astype(jnp.float32) * (
        2.0 * math.pi / SEG_LEN
    )
    taper = 0.5 - 0.5 * jnp.cos(sample.astype(jnp.float32) * (2.0 * math.pi / SEG_LEN))
    table = jnp.stack([taper[None, :] * jnp.cos(phase), -taper[None, :] * jnp.sin(phase)], axis=1)
    return table.reshape(2 * F, SEG_LEN).astype(jnp.bfloat16)


def lag_table():
    shifts = jnp.arange(NLAG, dtype=jnp.int32) - NLAG // 2
    bins = jnp.arange(F, dtype=jnp.int32) + LOW_BIN
    phase = (bins[:, None] * shifts[None, :] % SEG_LEN).astype(jnp.float32) * (
        2.0 * math.pi / SEG_LEN
    )
    return jnp.stack([jnp.cos(phase), -jnp.sin(phase)], axis=1).astype(jnp.bfloat16)


def whiten(samples, starts, table):
    pieces = jax.vmap(lambda begin: lax.dynamic_slice_in_dim(samples, begin, SEG_LEN, 1))(starts)
    spectra = jnp.einsum("kn,sin->ksi", table, pieces, preferred_element_type=jnp.float32)
    spectra = spectra.reshape(F, 2, spectra.shape[1], spectra.shape[2])
    amplitude = jnp.sqrt(spectra[:, 0] * spectra[:, 0] + spectra[:, 1] * spectra[:, 1])
    level = jnp.mean(amplitude, axis=0) + EPS
    return (spectra / (amplitude + LEVEL * level)[:, None]).astype(jnp.bfloat16)


def slot_lags(left_block, right_block, count, same, weight, lagtab, scale):
    freqs, parts, segs, width = right_block.shape
    direct = left_block.reshape(freqs, parts * segs, count)
    turned = jnp.concatenate([left_block[:, 1], -left_block[:, 0]], axis=1)
    left_form = jnp.concatenate([direct, turned], axis=2)
    right_form = right_block.reshape(freqs, parts * segs, width)
    gram = lax.dot_general(
        left_form, right_form, (((1,), (1,)), ((0,), (0,))), preferred_element_type=jnp.float32
    ).astype(jnp.bfloat16)
    gram = gram.reshape(freqs, 2, count, width)
    lags = lax.dot_general(
        lagtab, gram, (((0, 1), (0, 1)), ((), ())), preferred_element_type=jnp.float32
    )
    total = jnp.transpose(lags, (1, 0, 2))
    rows = jnp.arange(count, dtype=jnp.int32)
    columns = jnp.arange(width, dtype=jnp.int32)
    keep = 1.0 - same * (rows[:, None] == columns[None, :]).astype(jnp.float32)
    return total * scale * keep[:, None, :] * weight


def shards(record, seg_starts, pair_blocks, pair_owner):
    width, block_len = record.shape
    seg_dev = seg_starts.shape[0]
    tm_index = lax.axis_index("tm")
    chan_index = lax.axis_index("chan")
    following = passed_along(record[:, :SEG_LEN], "tm", -1)
    extended = jnp.concatenate([record, following], axis=1)
    local_starts = seg_starts - tm_index * block_len
    table = transform_table()
    lagtab = lag_table()
    scale = 2.0 / math.sqrt(seg_dev * lax.axis_size("tm") * F)
    wanted = chan_index * SLOTS + jnp.arange(SLOTS, dtype=jnp.int32)
    match = (pair_owner[None, :] == wanted[:, None]).astype(jnp.int32)
    live = jnp.sum(match, axis=1).astype(jnp.float32)
    first = jnp.sum(match * pair_blocks[None, :, 0], axis=1)
    second = jnp.sum(match * pair_blocks[None, :, 1], axis=1)
    rows_dev = width // lax.axis_size("tm")
    own = whiten(extended, local_starts, table)
    nearby = []
    for offset in (1, -1, -2):
        nearby.append(passed_along(own, "chan", offset))
    blocks = [nearby[0], own, nearby[1], nearby[2]]
    stacked = jnp.stack(blocks, axis=0)
    same = (first == second).astype(jnp.float32)
    first_near = jnp.clip(first - chan_index + 1, 0, 3)
    second_near = jnp.clip(second - chan_index + 1, 0, 3)
    lefts = []
    rights = []
    for slot in range(SLOTS):
        lefts.append(lax.dynamic_index_in_dim(stacked, first_near[slot], 0, keepdims=False))
        rights.append(lax.dynamic_index_in_dim(stacked, second_near[slot], 0, keepdims=False))
    results = []
    for slot in range(SLOTS):
        results.append(
            slot_lags(
                lefts[slot],
                rights[slot],
                rows_dev * lax.axis_size("tm"),
                same[slot],
                live[slot],
                lagtab,
                scale,
            )
        )
    return lax.psum_scatter(
        jnp.stack(results, axis=1).astype(jnp.bfloat16), "tm", scatter_dimension=0, tiled=True
    )


def solution(mesh):
    in_specs = (P("chan", "tm"), P("tm"), P(), P())
    out_specs = P("tm", "chan", None, None)
    return jax.shard_map(shards, mesh=mesh, in_specs=in_specs, out_specs=out_specs, check_vma=False)
```

profile of v0, /device:TPU:1, one launch (start us, length us, event | category | flops | bytes accessed | tf_op | source)
XLA Modules:
  0.0 427.9 jit_solution(7675730134899405460)
XLA Ops:
  6.5 0.9 slice.89
  7.5 1.3 collective-permute-start
  9.5 0.8 slice_bitcast_fusion.1
  10.3 3.1 multiply_convert_fusion.1
  13.4 1.3 fusion.73
  15.2 1.4 pad_maximum_fusion.2
  16.6 22.0 %while.1 = (s32[]{:T(128)}, bf16[128,4608]{1,0:T(8,128)(2,1)S(1)}, s32[16,2]{0,1:T(2,128)S(1)}, bf16[16,128,512]{2,1,0:T(8,128)(2,1)S(1)}, s32[]{:T(128)}) while((s32[]{:T(128)}, bf16[128,4608]{1,0:T(8,128)(2,1)S(1)}, s32[16,2]{0,1:T(2,128)S(1)}, bf16[16,128,512]{2,1,0:T(8,128)(2,1)S(1)}, s32[]{:T(128)}) %tuple.46), condition=%wide.while_cond, body=%wide.while_body.sunk | while | flops 2 | bytes 262241 | solution.py:46
  17.2 0.7 bitcast_dynamic-update-slice_fusion.2
  18.6 0.7 bitcast_dynamic-update-slice_fusion.2
  21.4 0.7 bitcast_dynamic-update-slice_fusion.2
  22.7 0.7 bitcast_dynamic-update-slice_fusion.2
  24.1 0.7 bitcast_dynamic-update-slice_fusion.2
  25.5 0.7 bitcast_dynamic-update-slice_fusion.2
  28.2 0.7 bitcast_dynamic-update-slice_fusion.2
  29.6 0.7 bitcast_dynamic-update-slice_fusion.2
  38.6 2.2 fusion.46
  40.8 0.8 fusion.68
  41.7 0.8 add_bitcast_fusion
  42.8 1.9 divide_convert_fusion
  44.7 4.5 %collective-permute-start.1 = (bf16[256,2,16,128]{0,3,2,1:T(8,128)(2,1)}, bf16[256,2,16,128]{0,3,2,1:T(8,128)(2,1)}, u32[]{:S(2)}, u32[]{:S(2)}) collective-permute-start(bf16[256,2,16,128]{0,3,2,1:T(8,128)(2,1)} %divide_convert_fusion), channel_id=1, source_target_pairs={{0,4},{4,8},{8,12},{12,16},{16,20},{20,24},{24,28},{28,32},{32,36}... | collective-permute-start | bytes 6291464 | tf_op jit(solution)/shard_map/ppermute | solution.py:22
  49.2 1.9 collective-permute-start.2
  51.1 1.3 collective-permute-start.3
  72.7 2.7 fusion.94
  75.4 22.5 %collective-permute-done.2 = bf16[256,2,16,128]{0,3,2,1:T(8,128)(2,1)} collective-permute-done((bf16[256,2,16,128]{0,3,2,1:T(8,128)(2,1)}, bf16[256,2,16,128]{0,3,2,1:T(8,128)(2,1)}, u32[]{:S(2)}, u32[]{:S(2)}) %collective-permute-start.2) | collective-permute-done | bytes 2097184 | tf_op jit(solution)/shard_map/ppermute | solution.py:22
  98.0 3.1 collective-permute-done.3
  101.1 4.3 %pad_maximum_fusion = bf16[4,256,2,16,128]{1,4,3,2,0:T(8,128)(2,1)S(1)} fusion(bf16[1,256,2,16,128]{1,4,3,2,0:T(8,128)(2,1)} %bitcast.9, bf16[1,256,2,16,128]{1,4,3,2,0:T(8,128)(2,1)} %bitcast.8, bf16[1,256,2,16,128]{1,4,3,2,0:T(8,128)(2,1)S(1)} %fusion.94, bf16[1,256,2,16,128]{1,4,3,2,0:T(8,128)(2,1)} %bitcast.6), kind=kLoop, calls=%fused_computation.15 | loop fusion | flops 12582912 | bytes 16777216 | tf_op jit(solution)/shard_map/stack | solution.py:96
  105.4 5.3 %constant_dynamic-slice_fusion.8 = (bf16[1,256,2,16,128]{1,4,3,2,0:T(8,128)(2,1)}, bf16[1,256,2,16,128]{1,4,3,2,0:T(8,128)(2,1)}, bf16[1,256,2,16,128]{1,4,3,2,0...) fusion(bf16[4,256,2,16,128]{1,4,3,2,0:T(8,128)(2,1)S(1)} %pad_m, ...), kind=kLoop, calls=%fused_computation.113 | loop fusion | bytes 33554464 | tf_op jit(solution)/shard_map/jit(dynamic_index_in_dim)/dynamic_slice | solution.py:103
  110.7 4.5 %copy.60 = bf16[1,256,2,16,128]{4,3,2,1,0:T(8,128)(2,1)} copy(bf16[1,256,2,16,128]{1,4,3,2,0:T(8,128)(2,1)} %get-tuple-element.24) | data formatting | bytes 4194304 | tf_op jit(solution)/shard_map/jit(dynamic_index_in_dim)/dynamic_slice | solution.py:103
  115.2 3.2 fusion.82
  118.4 1.9 copy.101
  120.3 1.1 negate_bitcast_fusion.3
  121.4 2.6 copy.100
  124.1 4.6 %copy.64 = bf16[1,256,2,16,128]{4,3,2,1,0:T(8,128)(2,1)} copy(bf16[1,256,2,16,128]{1,4,3,2,0:T(8,128)(2,1)} %get-tuple-element.31) | data formatting | bytes 4194304 | tf_op jit(solution)/shard_map/jit(dynamic_index_in_dim)/dynamic_slice | solution.py:104
  128.7 4.5 %copy.66 = bf16[1,256,2,16,128]{4,3,2,1,0:T(8,128)(2,1)} copy(bf16[1,256,2,16,128]{1,4,3,2,0:T(8,128)(2,1)} %get-tuple-element.30) | data formatting | bytes 4194304 | tf_op jit(solution)/shard_map/jit(dynamic_index_in_dim)/dynamic_slice | solution.py:103
  133.2 3.1 fusion.83
  136.3 1.9 copy.103
  138.2 1.1 negate_bitcast_fusion.2
  139.4 2.6 copy.102
  142.0 4.6 %copy.70 = bf16[1,256,2,16,128]{4,3,2,1,0:T(8,128)(2,1)} copy(bf16[1,256,2,16,128]{1,4,3,2,0:T(8,128)(2,1)} %get-tuple-element.29) | data formatting | bytes 4194304 | tf_op jit(solution)/shard_map/jit(dynamic_index_in_dim)/dynamic_slice | solution.py:104
  146.6 4.6 %copy.72 = bf16[1,256,2,16,128]{4,3,2,1,0:T(8,128)(2,1)} copy(bf16[1,256,2,16,128]{1,4,3,2,0:T(8,128)(2,1)} %get-tuple-element.28) | data formatting | bytes 4194304 | tf_op jit(solution)/shard_map/jit(dynamic_index_in_dim)/dynamic_slice | solution.py:103
  151.2 3.1 fusion.84
  154.2 1.9 copy.105
  156.2 1.1 negate_bitcast_fusion.1
  157.3 2.6 copy.104
  159.9 4.6 %copy.76 = bf16[1,256,2,16,128]{4,3,2,1,0:T(8,128)(2,1)} copy(bf16[1,256,2,16,128]{1,4,3,2,0:T(8,128)(2,1)} %get-tuple-element.27) | data formatting | bytes 4194304 | tf_op jit(solution)/shard_map/jit(dynamic_index_in_dim)/dynamic_slice | solution.py:104
  164.5 3.1 copy.78
  167.6 1.5 fusion.85
  169.1 1.9 copy.107
  171.1 1.1 negate_bitcast_fusion
  172.2 2.8 copy.106
  174.9 4.5 %copy.82 = bf16[1,256,2,16,128]{4,3,2,1,0:T(8,128)(2,1)} copy(bf16[1,256,2,16,128]{1,4,3,2,0:T(8,128)(2,1)} %get-tuple-element.25) | data formatting | bytes 4194304 | tf_op jit(solution)/shard_map/jit(dynamic_index_in_dim)/dynamic_slice | solution.py:104
  179.5 9.7 %convolution_convert_fusion.3 = bf16[256,256,128]{2,1,0:T(8,128)(2,1)} fusion(bf16[256,32,128]{2,1,0:T(8,128)(2,1)S(1)} %bitcast.163, bf16[256,16,128]{2,1,0:T(8,128)(2,1)S(1)} %copy-done.8, bf16[256,16,128]{2,1,0:T(8,128)(2,1)} %bitcast.171, bf16[256,32,128]{2,1,0:T(8,128)(2,1)} %bitcast.167), kind=kOutput, calls=%fused_computation.13 | convolution fusion | flops 557842432 | bytes 23068672 | tf_op jit(solution)/shard_map/dot_general | solution.py:60
  189.2 8.3 %convolution_convert_fusion.2 = bf16[256,256,128]{2,1,0:T(8,128)(2,1)} fusion(bf16[256,32,128]{2,1,0:T(8,128)(2,1)S(1)} %bitcast.164, bf16[256,16,128]{2,1,0:T(8,128)(2,1)S(1)} %copy-done.9, bf16[256,16,128]{2,1,0:T(8,128)(2,1)S(1)} %bitcast.172, bf16[256,32,128]{2,1,0:T(8,128)(2,1)S(1)} %bitcast.168), kind=kOutput, calls=%fused_computation.12 | convolution fusion | flops 557842432 | bytes 23068672 | tf_op jit(solution)/shard_map/dot_general | solution.py:60
  197.5 16.3 %fusion.48 = bf16[128,1,64,128]{3,2,0,1:T(8,128)(2,1)S(1)} fusion(f32[]{:T(128)} %bitcast.25, f32[128,128]{1,0:T(8,128)S(1)} %subtract_multiply_fusion.3, bf16[256,2,128,128]{3,2,1,0:T(8,128)(2,1)} %bitcast.153, bf16[256,1,64]{0,2,1:T(8,128)(2,1)S(1)} %get-tuple-element.41, bf16[256,1,64]{0,2,1:T(8,128)(2,1)S(1)} %get-tuple-element.40), kind=kOutput, calls=%fused_computation.57 | convolution fusion | flops 1077018624 | bytes 19005444 | tf_op jit(solution)/shard_map/dot_general | solution.py:64
  213.9 17.1 %fusion.51 = bf16[128,1,64,128]{3,2,0,1:T(8,128)(2,1)S(1)} fusion(f32[]{:T(128)} %bitcast.41, f32[128,128]{1,0:T(8,128)S(1)} %subtract_multiply_fusion.2, bf16[256,2,128,128]{3,2,1,0:T(8,128)(2,1)} %bitcast.154, bf16[256,1,64]{0,2,1:T(8,128)(2,1)S(1)} %get-tuple-element.41, bf16[256,1,64]{0,2,1:T(8,128)(2,1)S(1)} %get-tuple-element.40), kind=kOutput, calls=%fused_computation.58 | convolution fusion | flops 1077018624 | bytes 19005444 | tf_op jit(solution)/shard_map/dot_general | solution.py:64
  231.0 8.6 %convolution_convert_fusion.1 = bf16[256,256,128]{2,1,0:T(8,128)(2,1)} fusion(bf16[256,32,128]{2,1,0:T(8,128)(2,1)S(1)} %bitcast.165, bf16[256,16,128]{2,1,0:T(8,128)(2,1)S(1)} %copy-done.10, bf16[256,16,128]{2,1,0:T(8,128)(2,1)S(1)} %bitcast.173, bf16[256,32,128]{2,1,0:T(8,128)(2,1)S(1)} %bitcast.169), kind=kOutput, calls=%fused_computation.11 | convolution fusion | flops 557842432 | bytes 23068672 | tf_op jit(solution)/shard_map/dot_general | solution.py:60
  239.6 18.1 %fusion.54 = bf16[128,1,64,128]{3,2,0,1:T(8,128)(2,1)} fusion(f32[]{:T(128)} %bitcast.57, f32[128,128]{1,0:T(8,128)S(1)} %subtract_multiply_fusion.1, bf16[256,2,128,128]{3,2,1,0:T(8,128)(2,1)} %bitcast.156, bf16[256,1,64]{0,2,1:T(8,128)(2,1)S(1)} %get-tuple-element.41, bf16[256,1,64]{0,2,1:T(8,128)(2,1)S(1)} %get-tuple-element.40), kind=kOutput, calls=%fused_computation.59 | convolution fusion | flops 1077018624 | bytes 19005444 | tf_op jit(solution)/shard_map/dot_general | solution.py:64
  257.7 8.3 %convolution_convert_fusion = bf16[256,256,128]{2,1,0:T(8,128)(2,1)} fusion(bf16[256,32,128]{2,1,0:T(8,128)(2,1)S(1)} %bitcast.166, bf16[256,16,128]{2,1,0:T(8,128)(2,1)S(1)} %copy-done.13, bf16[256,16,128]{2,1,0:T(8,128)(2,1)S(1)} %bitcast.174, bf16[256,32,128]{2,1,0:T(8,128)(2,1)S(1)} %bitcast.170), kind=kOutput, calls=%fused_computation.10 | convolution fusion | flops 557842432 | bytes 23068672 | tf_op jit(solution)/shard_map/dot_general | solution.py:60
  266.1 16.5 %fusion.57 = bf16[128,1,64,128]{3,2,0,1:T(8,128)(2,1)S(1)} fusion(f32[]{:T(128)} %bitcast.73, f32[128,128]{1,0:T(8,128)S(1)} %subtract_multiply_fusion, bf16[256,2,128,128]{3,2,1,0:T(8,128)(2,1)} %bitcast.155, bf16[256,1,64]{0,2,1:T(8,128)(2,1)S(1)} %get-tuple-element.41, bf16[256,1,64]{0,2,1:T(8,128)(2,1)S(1)} %get-tuple-element.40), kind=kOutput, calls=%fused_computation.60 | convolution fusion | flops 1077018624 | bytes 19005444 | tf_op jit(solution)/shard_map/dot_general | solution.py:64
  282.6 4.1 pad_maximum_fusion.1
  286.7 9.7 %copy.98 = bf16[128,4,64,128]{3,2,1,0:T(8,128)(2,1)} copy(bf16[128,4,64,128]{3,2,0,1:T(8,128)(2,1)} %pad_maximum_fusion.1) | data formatting | bytes 16777216
  296.4 13.7 %copy.135 = bf16[16,8,256,128]{3,1,2,0:T(8,128)(2,1)} copy(bf16[16,8,256,128]{3,2,1,0:T(8,128)(2,1)} %bitcast.158) | data formatting | bytes 16777216
  310.1 107.3 %reduce-scatter.5.cloned.1.call-done = bf16[32,32768]{1,0:T(8,128)(2,1)} async-done(((bf16[128,32768]{1,0:T(8,128)(2,1)}), bf16[32,32768]{1,0:T(8,128)(2,1)}) %reduce-scatter.5.cloned.1.call-update) | async-done | bytes 2097168
  417.4 3.4 copy.109
  (106 shorter events, 22.7 us)
Async XLA Ops:
  6.5 410.9 %reduce-scatter.5.cloned.1.call-start = ((), (), s32[]{:S(2)}) async-start(), calls=%async_computation.1 | async-start | bytes 10485760
  7.5 7.8 %collective-permute-start = (bf16[128,512]{1,0:T(8,128)(2,1)S(1)}, bf16[128,512]{1,0:T(8,128)(2,1)}, u32[]{:S(2)}, u32[]{:S(2)}) collective-permute-start(bf16[128,512]{1,0:T(8,128)(2,1)S(1)} %slice.89), channel_id=1, source_target_pairs={{1,0},{2,1},{3,2},{5,4},{6,5},{7,6},{9,8},{10,9},{11,10},{13,12},{... | collective-permute-start | bytes 393224 | tf_op jit(solution)/shard_map/ppermute | solution.py:22
  14.7 0.5 copy-start.16
  14.7 0.5 copy-start.18
  40.8 2.0 copy-start
  42.8 20.8 %copy-start.20 = (s32[4]{0:T(128)S(1)}, s32[4]{0:T(128)}, u32[]{:S(2)}) copy-start(s32[4]{0:T(128)} %get-tuple-element.14) | copy-start | bytes 52
  42.8 25.8 %copy-start.17 = (s32[4]{0:T(128)S(1)}, s32[4]{0:T(128)}, u32[]{:S(2)}) copy-start(s32[4]{0:T(128)} %copy-done.16) | copy-start | bytes 52
  42.8 25.8 %copy-start.19 = (s32[4]{0:T(128)S(1)}, s32[4]{0:T(128)}, u32[]{:S(2)}) copy-start(s32[4]{0:T(128)} %copy-done.18) | copy-start | bytes 52
  44.7 30.7 %collective-permute-start.1 = (bf16[256,2,16,128]{0,3,2,1:T(8,128)(2,1)}, bf16[256,2,16,128]{0,3,2,1:T(8,128)(2,1)}, u32[]{:S(2)}, u32[]{:S(2)}) collective-permute-start(bf16[256,2,16,128]{0,3,2,1:T(8,128)(2,1)} %divide_convert_fusion), channel_id=1, source_target_pairs={{0,4},{4,8},{8,12},{12,16},{16,20},{20,24},{24,28},{28,32},{32,36}... | collective-permute-start | bytes 6291464 | tf_op jit(solution)/shard_map/ppermute | solution.py:22
  49.2 48.7 %collective-permute-start.2 = (bf16[256,2,16,128]{0,3,2,1:T(8,128)(2,1)}, bf16[256,2,16,128]{0,3,2,1:T(8,128)(2,1)}, u32[]{:S(2)}, u32[]{:S(2)}) collective-permute-start(bf16[256,2,16,128]{0,3,2,1:T(8,128)(2,1)} %divide_convert_fusion), channel_id=1, source_target_pairs={{4,0},{8,4},{12,8},{16,12},{20,16},{24,20},{28,24},{32,28},{36,32}... | collective-permute-start | bytes 6291464 | tf_op jit(solution)/shard_map/ppermute | solution.py:22
  51.1 49.9 %collective-permute-start.3 = (bf16[256,2,16,128]{0,3,2,1:T(8,128)(2,1)}, bf16[256,2,16,128]{0,3,2,1:T(8,128)(2,1)}, u32[]{:S(2)}, u32[]{:S(2)}) collective-permute-start(bf16[256,2,16,128]{0,3,2,1:T(8,128)(2,1)} %divide_convert_fusion), channel_id=1, source_target_pairs={{8,0},{12,4},{16,8},{20,12},{24,16},{28,20},{32,24},{36,28},{40,32... | collective-permute-start | bytes 6291464 | tf_op jit(solution)/shard_map/ppermute | solution.py:22
  171.1 8.4 %copy-start.1 = (bf16[1,256,2,16,128]{4,3,2,1,0:T(8,128)(2,1)S(1)}, bf16[1,256,2,16,128]{4,3,2,1,0:T(8,128)(2,1)}, u32[]{:S(2)}) copy-start(bf16[1,256,2,16,128]{4,3,2,1,0:T(8,128)(2,1)} %copy.64) | copy-start | bytes 6291460
  172.2 7.3 %copy-start.8 = (bf16[256,16,128]{2,1,0:T(8,128)(2,1)S(1)}, bf16[256,16,128]{2,1,0:T(8,128)(2,1)}, u32[]{:S(2)}) copy-start(bf16[256,16,128]{2,1,0:T(8,128)(2,1)} %negate_bitcast_fusion.3) | copy-start | bytes 3145732
  179.4 9.7 %copy-start.2 = (bf16[1,256,2,16,128]{4,3,2,1,0:T(8,128)(2,1)S(1)}, bf16[1,256,2,16,128]{4,3,2,1,0:T(8,128)(2,1)}, u32[]{:S(2)}) copy-start(bf16[1,256,2,16,128]{4,3,2,1,0:T(8,128)(2,1)} %copy.70) | copy-start | bytes 6291460
  179.4 9.7 %copy-start.5 = (bf16[1,256,2,16,128]{4,3,2,1,0:T(8,128)(2,1)S(1)}, bf16[1,256,2,16,128]{4,3,2,1,0:T(8,128)(2,1)}, u32[]{:S(2)}) copy-start(bf16[1,256,2,16,128]{4,3,2,1,0:T(8,128)(2,1)} %copy.66) | copy-start | bytes 6291460
  179.4 9.7 %copy-start.9 = (bf16[256,16,128]{2,1,0:T(8,128)(2,1)S(1)}, bf16[256,16,128]{2,1,0:T(8,128)(2,1)}, u32[]{:S(2)}) copy-start(bf16[256,16,128]{2,1,0:T(8,128)(2,1)} %negate_bitcast_fusion.2) | copy-start | bytes 3145732
  179.5 9.7 %copy-start.11 = (bf16[256,1,16,128]{3,2,0,1:T(8,128)(2,1)S(1)}, bf16[256,1,16,128]{3,2,0,1:T(8,128)(2,1)}, u32[]{:S(2)}) copy-start(bf16[256,1,16,128]{3,2,0,1:T(8,128)(2,1)} %copy.102) | copy-start | bytes 3145732
  213.8 17.1 %copy-start.3 = (bf16[1,256,2,16,128]{4,3,2,1,0:T(8,128)(2,1)S(1)}, bf16[1,256,2,16,128]{4,3,2,1,0:T(8,128)(2,1)}, u32[]{:S(2)}) copy-start(bf16[1,256,2,16,128]{4,3,2,1,0:T(8,128)(2,1)} %copy.76) | copy-start | bytes 6291460
  213.8 17.1 %copy-start.6 = (bf16[1,256,2,16,128]{4,3,2,1,0:T(8,128)(2,1)S(1)}, bf16[1,256,2,16,128]{4,3,2,1,0:T(8,128)(2,1)}, u32[]{:S(2)}) copy-start(bf16[1,256,2,16,128]{4,3,2,1,0:T(8,128)(2,1)} %copy.72) | copy-start | bytes 6291460
  213.8 17.1 %copy-start.10 = (bf16[256,16,128]{2,1,0:T(8,128)(2,1)S(1)}, bf16[256,16,128]{2,1,0:T(8,128)(2,1)}, u32[]{:S(2)}) copy-start(bf16[256,16,128]{2,1,0:T(8,128)(2,1)} %negate_bitcast_fusion.1) | copy-start | bytes 3145732
  213.9 17.1 %copy-start.12 = (bf16[256,1,16,128]{3,2,0,1:T(8,128)(2,1)S(1)}, bf16[256,1,16,128]{3,2,0,1:T(8,128)(2,1)}, u32[]{:S(2)}) copy-start(bf16[256,1,16,128]{3,2,0,1:T(8,128)(2,1)} %copy.104) | copy-start | bytes 3145732
  239.6 18.2 %copy-start.4 = (bf16[1,256,2,16,128]{4,3,2,1,0:T(8,128)(2,1)S(1)}, bf16[1,256,2,16,128]{4,3,2,1,0:T(8,128)(2,1)}, u32[]{:S(2)}) copy-start(bf16[1,256,2,16,128]{4,3,2,1,0:T(8,128)(2,1)} %copy.82) | copy-start | bytes 6291460
  239.6 18.2 %copy-start.7 = (bf16[1,256,2,16,128]{4,3,2,1,0:T(8,128)(2,1)S(1)}, bf16[1,256,2,16,128]{4,3,2,1,0:T(8,128)(2,1)}, u32[]{:S(2)}) copy-start(bf16[1,256,2,16,128]{4,3,2,1,0:T(8,128)(2,1)} %copy.78) | copy-start | bytes 6291460
  239.6 18.1 %copy-start.13 = (bf16[256,16,128]{2,1,0:T(8,128)(2,1)S(1)}, bf16[256,16,128]{2,1,0:T(8,128)(2,1)}, u32[]{:S(2)}) copy-start(bf16[256,16,128]{2,1,0:T(8,128)(2,1)} %negate_bitcast_fusion) | copy-start | bytes 3145732
  239.6 18.1 %copy-start.14 = (bf16[256,1,16,128]{3,2,0,1:T(8,128)(2,1)S(1)}, bf16[256,1,16,128]{3,2,0,1:T(8,128)(2,1)}, u32[]{:S(2)}) copy-start(bf16[256,1,16,128]{3,2,0,1:T(8,128)(2,1)} %copy.106) | copy-start | bytes 3145732
  266.1 16.5 %copy-start.15 = (bf16[128,1,64,128]{3,2,0,1:T(8,128)(2,1)S(1)}, bf16[128,1,64,128]{3,2,0,1:T(8,128)(2,1)}, u32[]{:S(2)}) copy-start(bf16[128,1,64,128]{3,2,0,1:T(8,128)(2,1)} %fusion.54) | copy-start | bytes 6291460
Sparse Core Ops, SparseCore 0:
  310.2 107.1 reduce-scatter.4
where the time goes:
time: 434 us; the launch traced here: 428 us
  waiting for transfers between devices  133 us (31%)
  local copies, waits for them, and re-layouts  123 us (28%)
  matrix products  105 us (24%)
  between operations  29 us (7%)
  other arithmetic  28.3 us (7%)
  starting transfers between devices  9.01 us (2%)
    unnamed x2, waiting for transfers between devices  107 us
    dot_general x4, matrix products, slot_lags(): lax.dot_general(lagtab, gram, (((0, 1), (0, 1)), ((), ())), preferred_ele...  68 us
    unnamed x53, local copies, waits for them, and re-layouts  46.1 us
    dot_general x4, matrix products, slot_lags(): lax.dot_general(left_form, right_form, (((1,), (1,)), ((0,), (0,))), pref...  34.9 us
    ppermute x4, waiting for transfers between devices, passed_along(): return lax.ppermute(block, axis, route)  25.6 us
    dynamic_slice x5, local copies, waits for them, and re-layouts, shards(): lax.dynamic_index_in_dim(stacked, first_near[slot], 0, keepdims=False)  22.1 us
    gather x48, local copies, waits for them, and re-layouts  21.6 us
    dynamic_slice x4, local copies, waits for them, and re-layouts, shards(): lax.dynamic_index_in_dim(stacked, second_near[slot], 0, keepdims=False)  18.2 us
  transfers between devices with their start and end apart: 5, of which 3 were waited for; matrix products, arithmetic and copies ran while one was open for 3% of the time, Pallas kernels for 0%

commit v1 on v0

v1 whole, which is shorter than its diff:
```python
import functools
import math

import jax
import jax.numpy as jnp
import numpy as np
from jax import lax
from jax.experimental import pallas as pl
from jax.experimental.pallas import tpu as pltpu
from jax.sharding import PartitionSpec as P

MESH = pl.DeviceIdType.MESH

SEG_LEN = 512
F = 256
LOW_BIN = 1
NLAG = 64
SLOTS = 4
LEVEL = 0.5
EPS = 1e-06

BLK = 128
SEGS_DEV = 16
GROUPS = F // 8
DEPTH = SEGS_DEV * 2 * 8
TILE = 32
HALF = TILE // 2
KINDS = 3
OPP, UP, DOWN, OWN = range(4)


def transform_table():
    sample = np.arange(SEG_LEN)
    bins = np.arange(F) + LOW_BIN
    phase = (bins[:, None] * sample[None, :] % SEG_LEN) * (2.0 * math.pi / SEG_LEN)
    taper = 0.5 - 0.5 * np.cos(sample * (2.0 * math.pi / SEG_LEN))
    table = np.concatenate([taper[None, :] * np.cos(phase), -taper[None, :] * np.sin(phase)], axis=0)
    return jnp.asarray(table.astype(np.float32)).astype(jnp.bfloat16)


def lag_table():
    shifts = np.arange(NLAG) - NLAG // 2
    bins = np.arange(F) + LOW_BIN
    phase = (bins[:, None] * shifts[None, :] % SEG_LEN) * (2.0 * math.pi / SEG_LEN)
    table = np.stack([np.cos(phase), -np.sin(phase)], axis=1).reshape(2 * F, NLAG)
    return jnp.asarray(np.ascontiguousarray(table.T).astype(np.float32)).astype(jnp.bfloat16)


def nt_dot(a, b):
    return lax.dot_general(a, b, (((1,), (1,)), ((), ())), preferred_element_type=jnp.float32)


def stacks_kernel(
    n_chan,
    n_tm,
    scale,
    starts_ref,
    record_ref,
    table_ref,
    lag_ref,
    out_ref,
    own_ext,
    next_ext,
    turned,
    spectra,
    expanded,
    gram,
    part,
    relay_up,
    relay_down,
    from_down,
    from_up,
    shared,
    local_sem,
    near_send,
    near_recv,
    sum_send,
    sum_recv,
):
    c = lax.axis_index("chan")
    z = lax.axis_index("tm")
    block_len = record_ref.shape[1]
    up = lax.rem(z + 1, n_tm)
    down = lax.rem(z + n_tm - 1, n_tm)
    c_next = lax.rem(c + 1, n_chan)
    c_prev = lax.rem(c + n_chan - 1, n_chan)
    c_next2 = lax.rem(c + 2, n_chan)
    c_prev2 = lax.rem(c + n_chan - 2, n_chan)
    odd = lax.rem(c, 2)
    mate = c + 1 - 2 * odd

    tiles = block_len // 128

    def load_copy(tile):
        columns = pl.ds(pl.multiple_of(tile * 128, 128), 128)
        return pltpu.make_async_copy(record_ref.at[:, columns], own_ext.at[tile], local_sem.at[tile])

    def start_load(tile, carry):
        load_copy(tile).start()
        return carry

    def wait_load(tile, carry):
        load_copy(tile).wait()
        return carry

    lax.fori_loop(0, tiles, start_load, 0)

    barrier = pltpu.get_barrier_semaphore()
    for who in ((c, up), (c, down), (c_next2, z), (c_next2, up), (mate, z), (c_prev, z)):
        pl.semaphore_signal(barrier, inc=1, device_id=who, device_id_type=MESH)
    pl.semaphore_wait(barrier, 6)

    def near(index, src, dst, who):
        return pltpu.make_async_remote_copy(
            src_ref=src,
            dst_ref=dst,
            send_sem=near_send.at[index],
            recv_sem=near_recv.at[index],
            device_id=who,
            device_id_type=MESH,
        )

    main, halo = pl.ds(0, tiles), pl.ds(tiles, SEG_LEN // 128)
    head = own_ext.at[pl.ds(0, SEG_LEN // 128)]
    own_halo = near(0, head, own_ext.at[halo], (c, down))
    next_halo = near(1, head, next_ext.at[halo], (c_prev2, down))
    next_main = near(2, own_ext.at[main], next_ext.at[main], (c_prev2, z))
    lax.fori_loop(0, tiles, wait_load, 0)
    own_halo.start()
    next_halo.start()
    next_main.start()

    def to_mate():
        return near(3, spectra.at[2 - 2 * odd], spectra.at[1], (mate, z))

    def forward():
        return near(4, out_ref.at[2], shared, (c_next, z))

    def sum_copies(kind):
        low, high = pl.ds(0, HALF), pl.ds(HALF, HALF)
        routes = (
            (part.at[kind, OPP, low], relay_up.at[kind], up),
            (part.at[kind, OPP, high], relay_down.at[kind], down),
            (part.at[kind, UP, high], from_down.at[kind, high], up),
            (part.at[kind, UP, low], from_down.at[kind, low], up),
            (part.at[kind, DOWN, low], from_up.at[kind, low], down),
            (part.at[kind, DOWN, high], from_up.at[kind, high], down),
        )
        return [
            pltpu.make_async_remote_copy(
                src_ref=src,
                dst_ref=dst,
                send_sem=sum_send.at[kind, index],
                recv_sem=sum_recv.at[kind, index],
                device_id=(c, who),
                device_id_type=MESH,
            )
            for index, (src, dst, who) in enumerate(routes)
        ]

    ahead = lax.broadcasted_iota(jnp.int32, (256, 128), 0) - lax.broadcasted_iota(jnp.int32, (256, 128), 1)

    def cut(ext, seg):
        start = lax.rem(starts_ref[seg], block_len)
        first = lax.shift_right_logical(start, 7)
        shift = jnp.where(ahead == start - first * 128, 1.0, 0.0).astype(jnp.bfloat16)
        tiles = [ext[first + j] for j in range(SEG_LEN // 128 + 1)]
        rows = jnp.concatenate(
            [jnp.concatenate([tiles[j], tiles[j + 1]], axis=1) for j in range(SEG_LEN // 128)], axis=0
        )
        moved = jnp.dot(rows, shift, preferred_element_type=jnp.float32).astype(jnp.bfloat16)
        return jnp.concatenate([moved[BLK * j : BLK * (j + 1)] for j in range(SEG_LEN // 128)], axis=1)

    def whiten(ext, kind, turn_too):
        def step(pair, carry):
            pieces = jnp.concatenate([cut(ext, 2 * pair), cut(ext, 2 * pair + 1)], axis=0)
            both = nt_dot(table_ref[...], pieces)
            for h in range(2):
                real = both[:F, BLK * h : BLK * (h + 1)]
                imag = both[F:, BLK * h : BLK * (h + 1)]
                amplitude = jnp.sqrt(real * real + imag * imag)
                level = jnp.mean(amplitude, axis=0, keepdims=True) + EPS
                inverse = 1.0 / (amplitude + LEVEL * level)
                real = (real * inverse).reshape(GROUPS, 8, BLK)
                imag = (imag * inverse).reshape(GROUPS, 8, BLK)
                rows = pl.ds(pl.multiple_of((2 * pair + h) * 16, 16), 16)
                spectra[kind, :, rows, :] = jnp.concatenate([real, imag], axis=1).astype(jnp.bfloat16)
                if turn_too:
                    turned[:, rows, :] = jnp.concatenate([imag, -real], axis=1).astype(jnp.bfloat16)
            return carry

        lax.fori_loop(0, SEGS_DEV // 2, step, 0)

    def dest(tile):
        return lax.rem(z + jnp.where(tile == OPP, 2, jnp.where(tile == UP, 1, jnp.where(tile == DOWN, n_tm - 1, 0))), n_tm)

    ROWS = TILE * 8

    def expand(tile):
        row = lax.broadcasted_iota(jnp.int32, (ROWS, DEPTH), 0)
        col = lax.broadcasted_iota(jnp.int32, (ROWS, DEPTH), 1)
        wanted = (row % 2) * BLK + dest(tile) * TILE + row // 8
        pick = jnp.where(col == wanted, 1.0, 0.0).astype(jnp.bfloat16)
        mask = jnp.where(col % 4 == (row // 2) % 4, 1.0, 0.0)

        def step(group, carry):
            both = jnp.concatenate([spectra[0, group], turned[group]], axis=1)
            expanded[tile, group] = (nt_dot(pick, both) * mask).astype(jnp.bfloat16)
            return carry

        lax.fori_loop(0, GROUPS, step, 0)

    def tile_lags(kind, tile):
        row = lax.broadcasted_iota(jnp.int32, (DEPTH, BLK), 0)
        first = jnp.where(row % 8 < 4, 1.0, 0.0).astype(jnp.bfloat16)
        second = jnp.where(row % 8 < 4, 0.0, 1.0).astype(jnp.bfloat16)

        def gram_step(group, carry):
            right = spectra[kind, group]
            weights = jnp.concatenate([right * first, right * second], axis=1)
            cross = jnp.dot(expanded[tile, group], weights, preferred_element_type=jnp.float32)
            cross = jnp.concatenate(
                [cross[:, :BLK].reshape(TILE, 8, BLK), cross[:, BLK:].reshape(TILE, 8, BLK)], axis=1
            )
            rows = pl.ds(pl.multiple_of(group * 16, 16), 16)
            gram[:, rows, :] = cross.astype(jnp.bfloat16)
            return carry

        lax.fori_loop(0, GROUPS, gram_step, 0)

        def lag_step(pair, carry):
            two = jnp.concatenate([gram[2 * pair], gram[2 * pair + 1]], axis=1)
            lags = jnp.dot(lag_ref[...], two, preferred_element_type=jnp.float32) * scale
            part[kind, tile, 2 * pair] = lags[:, :BLK].astype(jnp.bfloat16)
            part[kind, tile, 2 * pair + 1] = lags[:, BLK:].astype(jnp.bfloat16)
            return carry

        lax.fori_loop(0, TILE // 2, lag_step, 0)

    def relay(kind):
        copies = sum_copies(kind)

        def add(tile, first_row, held):
            def step(i, carry):
                total = part[kind, tile, first_row + i].astype(jnp.float32) + held[kind, i].astype(jnp.float32)
                part[kind, tile, first_row + i] = total.astype(jnp.bfloat16)
                return carry

            lax.fori_loop(0, HALF, step, 0)

        copies[0].wait_recv()
        add(UP, 0, relay_up)
        copies[3].start()
        copies[1].wait_recv()
        add(DOWN, HALF, relay_down)
        copies[5].start()

    def finish(kind):
        copies = sum_copies(kind)
        for index in (2, 3, 4, 5):
            copies[index].wait_recv()
        column = lax.broadcasted_iota(jnp.int32, (NLAG, BLK), 1)

        def step(i, carry):
            total = part[kind, OWN, i].astype(jnp.float32) + (
                from_down[kind, i].astype(jnp.float32) + from_up[kind, i].astype(jnp.float32)
            )
            drop = jnp.where(kind == 0, z * TILE + i, -1)
            out_ref[kind, i] = jnp.where(column == drop, 0.0, total).astype(jnp.bfloat16)
            return carry

        lax.fori_loop(0, TILE, step, 0)

        @pl.when(kind == 2)
        def _():
            forward().start()

    own_halo.wait()
    whiten(own_ext, 0, True)

    @pl.when(odd == 1)
    def _():
        to_mate().start()

    def kind_of(step):
        return lax.rem(step * (1 + odd), KINDS)

    def kind_step(step, carry):
        kind = kind_of(step)

        @pl.when(step == 2 - odd)
        def _():
            next_main.wait()
            next_halo.wait()
            whiten(next_ext, 2, False)

            @pl.when(odd == 0)
            def _():
                to_mate().start()

        @pl.when(kind == 1)
        def _():
            to_mate().wait_recv()

        def tile_step(tile, carry):
            @pl.when(step == 0)
            def _():
                expand(tile)

            tile_lags(kind, tile)
            copies = sum_copies(kind)

            @pl.when(tile == OPP)
            def _():
                copies[0].start()
                copies[1].start()

            @pl.when(tile == UP)
            def _():
                copies[2].start()

            @pl.when(tile == DOWN)
            def _():
                copies[4].start()

            return carry

        lax.fori_loop(0, 4, tile_step, 0)
        relay(kind)

        @pl.when(step > 0)
        def _():
            finish(kind_of(step - 1))

        return carry

    lax.fori_loop(0, KINDS, kind_step, 0)
    finish(kind_of(2))

    to_mate().wait_send()
    forward().wait_send()
    forward().wait_recv()
    for kind in range(KINDS):
        for copy in sum_copies(kind):
            copy.wait_send()
    out_ref[3] = shared[...]


def place_kernel(kinds_ref, live_ref, block_ref, out_ref):
    q = pl.program_id(0)

    @pl.when(live_ref[q] > 0)
    def _():
        out_ref[...] = block_ref[0]

    @pl.when(live_ref[q] == 0)
    def _():
        out_ref[...] = jnp.zeros_like(out_ref)


def shards(n_chan, n_tm, record, seg_starts, pair_blocks, pair_owner):
    block_len = record.shape[1]
    scale = 2.0 / math.sqrt(SEGS_DEV * n_tm * F)
    bf16 = jnp.bfloat16
    stacks = pl.pallas_call(
        functools.partial(stacks_kernel, n_chan, n_tm, scale),
        out_shape=jax.ShapeDtypeStruct((4, TILE, NLAG, BLK), bf16),
        in_specs=[
            pl.BlockSpec(memory_space=pltpu.SMEM),
            pl.BlockSpec(memory_space=pl.ANY),
            pl.BlockSpec(memory_space=pltpu.VMEM),
            pl.BlockSpec(memory_space=pltpu.VMEM),
        ],
        out_specs=pl.BlockSpec(memory_space=pltpu.VMEM),
        scratch_shapes=[
            pltpu.VMEM(((block_len + SEG_LEN) // 128, BLK, 128), bf16),
            pltpu.VMEM(((block_len + SEG_LEN) // 128, BLK, 128), bf16),
            pltpu.VMEM((GROUPS, DEPTH, BLK), bf16),
            pltpu.VMEM((KINDS, GROUPS, DEPTH, BLK), bf16),
            pltpu.VMEM((4, GROUPS, TILE * 8, DEPTH), bf16),
            pltpu.VMEM((TILE, 2 * F, BLK), bf16),
            pltpu.VMEM((KINDS, 4, TILE, NLAG, BLK), bf16),
            pltpu.VMEM((KINDS, HALF, NLAG, BLK), bf16),
            pltpu.VMEM((KINDS, HALF, NLAG, BLK), bf16),
            pltpu.VMEM((KINDS, TILE, NLAG, BLK), bf16),
            pltpu.VMEM((KINDS, TILE, NLAG, BLK), bf16),
            pltpu.VMEM((TILE, NLAG, BLK), bf16),
            pltpu.SemaphoreType.DMA((block_len // 128,)),
            pltpu.SemaphoreType.DMA((5,)),
            pltpu.SemaphoreType.DMA((5,)),
            pltpu.SemaphoreType.DMA((KINDS, 6)),
            pltpu.SemaphoreType.DMA((KINDS, 6)),
        ],
        compiler_params=pltpu.CompilerParams(
            collective_id=0, has_side_effects=True, vmem_limit_bytes=60 * 1024 * 1024
        ),
        name="stacks",
    )(seg_starts, record, transform_table(), lag_table())

    chan = lax.axis_index("chan")
    wanted = chan * SLOTS + jnp.arange(SLOTS, dtype=jnp.int32)
    match = (pair_owner[None, :] == wanted[:, None]).astype(jnp.int32)
    apart = pair_blocks[:, 1] - pair_blocks[:, 0]
    kind = jnp.where((apart == 2) & (pair_blocks[:, 0] != chan), 3, apart)
    live = jnp.sum(match, axis=1)
    kinds = jnp.sum(match * kind[None, :], axis=1)
    return pl.pallas_call(
        place_kernel,
        out_shape=jax.ShapeDtypeStruct((TILE, SLOTS, NLAG, BLK), bf16),
        grid_spec=pltpu.PrefetchScalarGridSpec(
            num_scalar_prefetch=2,
            grid=(SLOTS,),
            in_specs=[pl.BlockSpec((1, TILE, NLAG, BLK), lambda q, kinds, live: (kinds[q], 0, 0, 0))],
            out_specs=pl.BlockSpec((TILE, None, NLAG, BLK), lambda q, kinds, live: (0, q, 0, 0)),
        ),
        name="place",
    )(kinds, live, stacks)


def solution(mesh):
    in_specs = (P("chan", "tm"), P("tm"), P(), P())
    out_specs = P("tm", "chan", None, None)
    body = functools.partial(shards, mesh.shape["chan"], mesh.shape["tm"])
    return jax.shard_map(body, mesh=mesh, in_specs=in_specs, out_specs=out_specs, check_vma=False)
```

time: 434 us -> 186 us (0.43); the launches traced: 428 us -> 186 us
  Pallas kernels: 0 us -> 184 us
  waiting for transfers between devices: 133 us -> 0 us
  local copies, waits for them, and re-layouts: 123 us -> 0 us
  matrix products: 105 us -> 0 us
  between operations: 29 us -> 0.01 us
  other arithmetic: 28.3 us -> 2.18 us
  starting transfers between devices: 9.01 us -> 0 us
    pallas_call x0 -> x2, Pallas kernels: none -> 184 us  [the longest x1 179 us: shards(): pl.pallas_call(functools.partial(stacks_kernel, n_chan, n_tm, scale), out...]
    unnamed x2 -> x0, waiting for transfers between devices: 107 us -> none
    dot_general x9 -> x0, matrix products: 105 us -> none  [the longest x4 68 us: slot_lags(): lax.dot_general(lagtab, gram, (((0, 1), (0, 1)), ((), ())), preferred_ele...]
    unnamed x53 -> x0, local copies, waits for them, and re-layouts: 46.1 us -> none
    dynamic_slice x9 -> x0, local copies, waits for them, and re-layouts: 40.4 us -> none  [the longest x5 22.1 us: shards(): lax.dynamic_index_in_dim(stacked, first_near[slot], 0, keepdims=False)]
    ppermute x4 -> x0, waiting for transfers between devices: 25.6 us -> none  [passed_along(): return lax.ppermute(block, axis, route)]
    gather x48 -> x0, local copies, waits for them, and re-layouts: 21.6 us -> none
    another operation x5 -> x0, other arithmetic: 14.5 us -> none  [the longest x2 7.01 us: shards(): stacked = jnp.stack(blocks, axis=0)]
  transfers between devices with their start and end apart: 5 -> 0, of which waited for: 3 -> 0; matrix products, arithmetic and copies ran while one was open for 3% -> 0% of each run, Pallas kernels for 0% -> 0%
where the time goes in v1:
time: 186 us
  Pallas kernels  184 us (99%)
  other arithmetic  2.18 us (1%)
    pallas_call x1, Pallas kernels, shards(): pl.pallas_call(functools.partial(stacks_kernel, n_chan, n_tm, scale), out...  179 us
    pallas_call x1, Pallas kernels, shards(): pl.pallas_call(place_kernel, out_shape=jax.ShapeDtypeStruct((TILE, SLOTS,...  4.48 us

profile of v1, /device:TPU:1, one launch (start us, length us, event | category | flops | bytes accessed | tf_op | source)
XLA Modules:
  0.0 186.1 jit_solution(16392116958269785012)
XLA Ops:
  0.0 0.8 fusion.2
  0.8 1.4 fusion.1
  2.2 179.4 %stacks.1.block_ref = bf16[4,32,64,128]{3,2,1,0:T(8,128)(2,1)} custom-call(s32[16]{0:T(128)} %starts_ref.1, bf16[128,4096]{1,0:T(8,128)(2,1)} %record_ref.1, bf16[512,512]{1,0:T(8,128)(2,1)} %constant.21.table_ref, bf16[64,512]{1,0:T(8,128)(2,1)} %constant.22.lag_ref), custom_call_target="tpu_custom_call" | custom-call | tf_op jit(solution)/shard_map/stacks/pallas_call | solution.py:365
  181.6 4.5 %place.1 = bf16[32,4,64,128]{3,2,1,0:T(8,128)(2,1)} custom-call(s32[4]{0:T(128)} %get-tuple-element.6.kinds_ref, s32[4]{0:T(128)} %get-tuple-element.5.live_ref, bf16[4,32,64,128]{3,2,1,0:T(8,128)(2,1)} %stacks.1.block_ref), custom_call_target="tpu_custom_call" | custom-call | tf_op jit(solution)/shard_map/place/pallas_call | solution.py:407
  (1 shorter events, 0.0 us)

commit v2 on v1

--- a/solution.py
+++ b/solution.py
@@ -158,18 +158,20 @@
             for index, (src, dst, who) in enumerate(routes)
         ]
 
-    ahead = lax.broadcasted_iota(jnp.int32, (256, 128), 0) - lax.broadcasted_iota(jnp.int32, (256, 128), 1)
+    lane = lax.broadcasted_iota(jnp.int32, (BLK, 128), 1)
 
     def cut(ext, seg):
         start = lax.rem(starts_ref[seg], block_len)
         first = lax.shift_right_logical(start, 7)
-        shift = jnp.where(ahead == start - first * 128, 1.0, 0.0).astype(jnp.bfloat16)
-        tiles = [ext[first + j] for j in range(SEG_LEN // 128 + 1)]
-        rows = jnp.concatenate(
-            [jnp.concatenate([tiles[j], tiles[j + 1]], axis=1) for j in range(SEG_LEN // 128)], axis=0
-        )
-        moved = jnp.dot(rows, shift, preferred_element_type=jnp.float32).astype(jnp.bfloat16)
-        return jnp.concatenate([moved[BLK * j : BLK * (j + 1)] for j in range(SEG_LEN // 128)], axis=1)
+        rest = start - first * 128
+        turn = jnp.bitwise_and(128 - rest, 127)
+        cols = [
+            pltpu.roll(ext[first + j].astype(jnp.float32), turn, 1) for j in range(SEG_LEN // 128 + 1)
+        ]
+        inside = lane < 128 - rest
+        return jnp.concatenate(
+            [jnp.where(inside, cols[j], cols[j + 1]) for j in range(SEG_LEN // 128)], axis=1
+        ).astype(jnp.bfloat16)
 
     def whiten(ext, kind, turn_too):
         def step(pair, carry):
@@ -189,36 +191,47 @@
                     turned[:, rows, :] = jnp.concatenate([imag, -real], axis=1).astype(jnp.bfloat16)
             return carry
 
-        lax.fori_loop(0, SEGS_DEV // 2, step, 0)
+        lax.fori_loop(0, SEGS_DEV // 2, step, 0, unroll=4)
 
     def dest(tile):
-        return lax.rem(z + jnp.where(tile == OPP, 2, jnp.where(tile == UP, 1, jnp.where(tile == DOWN, n_tm - 1, 0))), n_tm)
-
-    ROWS = TILE * 8
-
-    def expand(tile):
-        row = lax.broadcasted_iota(jnp.int32, (ROWS, DEPTH), 0)
-        col = lax.broadcasted_iota(jnp.int32, (ROWS, DEPTH), 1)
-        wanted = (row % 2) * BLK + dest(tile) * TILE + row // 8
-        pick = jnp.where(col == wanted, 1.0, 0.0).astype(jnp.bfloat16)
-        mask = jnp.where(col % 4 == (row // 2) % 4, 1.0, 0.0)
+        ahead = jnp.where(tile == OPP, 2, jnp.where(tile == UP, 1, jnp.where(tile == DOWN, n_tm - 1, 0)))
+        return lax.rem(z + ahead, n_tm)
+
+    def expand():
+        row = lax.broadcasted_iota(jnp.int32, (8, DEPTH), 0)
+        col = lax.broadcasted_iota(jnp.int32, (8, DEPTH), 1)
+        mine = col % 4 == row // 2
+        direct_mask = jnp.where(mine & (row % 2 == 0), 1.0, 0.0).reshape(1, 8, DEPTH)
+        turned_mask = jnp.where(mine & (row % 2 == 1), 1.0, 0.0).reshape(1, 8, DEPTH)
+        eye_row = lax.broadcasted_iota(jnp.int32, (BLK, BLK), 0)
+        eye_col = lax.broadcasted_iota(jnp.int32, (BLK, BLK), 1)
+        eye = jnp.where(eye_row == eye_col, 1.0, 0.0).astype(jnp.bfloat16)
 
         def step(group, carry):
-            both = jnp.concatenate([spectra[0, group], turned[group]], axis=1)
-            expanded[tile, group] = (nt_dot(pick, both) * mask).astype(jnp.bfloat16)
-            return carry
-
-        lax.fori_loop(0, GROUPS, step, 0)
+            direct = nt_dot(eye, spectra[0, group])
+            turn = nt_dot(eye, turned[group])
+            for q in range(BLK // TILE):
+                rows = slice(q * TILE, (q + 1) * TILE)
+                both = (
+                    direct[rows].reshape(TILE, 1, DEPTH) * direct_mask
+                    + turn[rows].reshape(TILE, 1, DEPTH) * turned_mask
+                )
+                expanded[group, q * TILE * 8 : (q + 1) * TILE * 8] = both.reshape(TILE * 8, DEPTH).astype(jnp.bfloat16)
+            return carry
+
+        lax.fori_loop(0, GROUPS, step, 0, unroll=4)
 
     def tile_lags(kind, tile):
         row = lax.broadcasted_iota(jnp.int32, (DEPTH, BLK), 0)
         first = jnp.where(row % 8 < 4, 1.0, 0.0).astype(jnp.bfloat16)
         second = jnp.where(row % 8 < 4, 0.0, 1.0).astype(jnp.bfloat16)
 
+        left_rows = pl.ds(pl.multiple_of(dest(tile) * TILE * 8, TILE * 8), TILE * 8)
+
         def gram_step(group, carry):
             right = spectra[kind, group]
             weights = jnp.concatenate([right * first, right * second], axis=1)
-            cross = jnp.dot(expanded[tile, group], weights, preferred_element_type=jnp.float32)
+            cross = jnp.dot(expanded[group, left_rows], weights, preferred_element_type=jnp.float32)
             cross = jnp.concatenate(
                 [cross[:, :BLK].reshape(TILE, 8, BLK), cross[:, BLK:].reshape(TILE, 8, BLK)], axis=1
             )
@@ -226,7 +239,7 @@
             gram[:, rows, :] = cross.astype(jnp.bfloat16)
             return carry
 
-        lax.fori_loop(0, GROUPS, gram_step, 0)
+        lax.fori_loop(0, GROUPS, gram_step, 0, unroll=16)
 
         def lag_step(pair, carry):
             two = jnp.concatenate([gram[2 * pair], gram[2 * pair + 1]], axis=1)
@@ -235,7 +248,7 @@
             part[kind, tile, 2 * pair + 1] = lags[:, BLK:].astype(jnp.bfloat16)
             return carry
 
-        lax.fori_loop(0, TILE // 2, lag_step, 0)
+        lax.fori_loop(0, TILE // 2, lag_step, 0, unroll=16)
 
     def relay(kind):
         copies = sum_copies(kind)
@@ -246,7 +259,7 @@
                 part[kind, tile, first_row + i] = total.astype(jnp.bfloat16)
                 return carry
 
-            lax.fori_loop(0, HALF, step, 0)
+            lax.fori_loop(0, HALF, step, 0, unroll=4)
 
         copies[0].wait_recv()
         add(UP, 0, relay_up)
@@ -269,7 +282,7 @@
             out_ref[kind, i] = jnp.where(column == drop, 0.0, total).astype(jnp.bfloat16)
             return carry
 
-        lax.fori_loop(0, TILE, step, 0)
+        lax.fori_loop(0, TILE, step, 0, unroll=4)
 
         @pl.when(kind == 2)
         def _():
@@ -281,6 +294,8 @@
     @pl.when(odd == 1)
     def _():
         to_mate().start()
+
+    expand()
 
     def kind_of(step):
         return lax.rem(step * (1 + odd), KINDS)
@@ -303,10 +318,6 @@
             to_mate().wait_recv()
 
         def tile_step(tile, carry):
-            @pl.when(step == 0)
-            def _():
-                expand(tile)
-
             tile_lags(kind, tile)
             copies = sum_copies(kind)
 
@@ -377,7 +388,7 @@
             pltpu.VMEM(((block_len + SEG_LEN) // 128, BLK, 128), bf16),
             pltpu.VMEM((GROUPS, DEPTH, BLK), bf16),
             pltpu.VMEM((KINDS, GROUPS, DEPTH, BLK), bf16),
-            pltpu.VMEM((4, GROUPS, TILE * 8, DEPTH), bf16),
+            pltpu.VMEM((GROUPS, BLK * 8, DEPTH), bf16),
             pltpu.VMEM((TILE, 2 * F, BLK), bf16),
             pltpu.VMEM((KINDS, 4, TILE, NLAG, BLK), bf16),
             pltpu.VMEM((KINDS, HALF, NLAG, BLK), bf16),

time: 186 us -> 94 us (0.51)
  Pallas kernels: 184 us -> 91.5 us
    pallas_call x1, Pallas kernels: 179 us -> 87 us  [shards(): pl.pallas_call(functools.partial(stacks_kernel, n_chan, n_tm, scale), out...]
where the time goes in v2:
time: 94 us; the launch traced here: 93.7 us
  Pallas kernels  91.5 us (97%)
  other arithmetic  2.18 us (2%)
    pallas_call x1, Pallas kernels, shards(): pl.pallas_call(functools.partial(stacks_kernel, n_chan, n_tm, scale), out...  87 us
    pallas_call x1, Pallas kernels, shards(): pl.pallas_call(place_kernel, out_shape=jax.ShapeDtypeStruct((TILE, SLOTS,...  4.48 us

profile of v2, /device:TPU:1, one launch (start us, length us, event | category | flops | bytes accessed | tf_op | source)
XLA Modules:
  0.0 93.7 jit_solution(9211435810017621421)
XLA Ops:
  0.0 0.8 fusion.2
  0.8 1.4 %fusion.1 = (s32[4]{0:T(128)}, s32[4]{0:T(128)}) fusion(s32[93]{0:T(128)} %param.9, s32[4]{0:T(128)S(1)} %iota_add_fusion, s32[93]{0:T(128)S(1)} %fusion.2), kind=kLoop, calls=%fused_computation.3 | loop fusion | flops 1852 | bytes 792 | tf_op jit(solution)/shard_map/reduce_sum | solution.py:416
  2.2 87.0 %stacks.1.block_ref = bf16[4,32,64,128]{3,2,1,0:T(8,128)(2,1)} custom-call(s32[16]{0:T(128)} %starts_ref.1, bf16[128,4096]{1,0:T(8,128)(2,1)} %record_ref.1, bf16[512,512]{1,0:T(8,128)(2,1)} %constant.21.table_ref, bf16[64,512]{1,0:T(8,128)(2,1)} %constant.22.lag_ref), custom_call_target="tpu_custom_call" | custom-call | tf_op jit(solution)/shard_map/stacks/pallas_call | solution.py:376
  89.2 4.5 %place.1 = bf16[32,4,64,128]{3,2,1,0:T(8,128)(2,1)} custom-call(s32[4]{0:T(128)} %get-tuple-element.6.kinds_ref, s32[4]{0:T(128)} %get-tuple-element.5.live_ref, bf16[4,32,64,128]{3,2,1,0:T(8,128)(2,1)} %stacks.1.block_ref), custom_call_target="tpu_custom_call" | custom-call | tf_op jit(solution)/shard_map/place/pallas_call | solution.py:418
  (1 shorter events, 0.0 us)

commit v3 on v2

--- a/solution.py
+++ b/solution.py
@@ -55,13 +55,18 @@
     n_tm,
     scale,
     starts_ref,
+    blocks_ref,
+    owner_ref,
     record_ref,
-    table_ref,
+    table_hbm,
     lag_ref,
     out_ref,
+    kinds_ref,
+    table_ref,
     own_ext,
     next_ext,
     turned,
+    sides,
     spectra,
     expanded,
     gram,
@@ -70,8 +75,10 @@
     relay_down,
     from_down,
     from_up,
-    shared,
+    done,
     local_sem,
+    table_sem,
+    done_sem,
     near_send,
     near_recv,
     sum_send,
@@ -104,6 +111,8 @@
         return carry
 
     lax.fori_loop(0, tiles, start_load, 0)
+    table_copy = pltpu.make_async_copy(table_hbm, table_ref, table_sem)
+    table_copy.start()
 
     barrier = pltpu.get_barrier_semaphore()
     for who in ((c, up), (c, down), (c_next2, z), (c_next2, up), (mate, z), (c_prev, z)):
@@ -134,7 +143,10 @@
         return near(3, spectra.at[2 - 2 * odd], spectra.at[1], (mate, z))
 
     def forward():
-        return near(4, out_ref.at[2], shared, (c_next, z))
+        return near(4, done.at[2], out_ref.at[3], (c_next, z))
+
+    def store(kind):
+        return pltpu.make_async_copy(done.at[kind], out_ref.at[kind], done_sem.at[kind])
 
     def sum_copies(kind):
         low, high = pl.ds(0, HALF), pl.ds(HALF, HALF)
@@ -197,49 +209,61 @@
         ahead = jnp.where(tile == OPP, 2, jnp.where(tile == UP, 1, jnp.where(tile == DOWN, n_tm - 1, 0)))
         return lax.rem(z + ahead, n_tm)
 
-    def expand():
-        row = lax.broadcasted_iota(jnp.int32, (8, DEPTH), 0)
-        col = lax.broadcasted_iota(jnp.int32, (8, DEPTH), 1)
-        mine = col % 4 == row // 2
-        direct_mask = jnp.where(mine & (row % 2 == 0), 1.0, 0.0).reshape(1, 8, DEPTH)
-        turned_mask = jnp.where(mine & (row % 2 == 1), 1.0, 0.0).reshape(1, 8, DEPTH)
+    def transpose():
         eye_row = lax.broadcasted_iota(jnp.int32, (BLK, BLK), 0)
         eye_col = lax.broadcasted_iota(jnp.int32, (BLK, BLK), 1)
         eye = jnp.where(eye_row == eye_col, 1.0, 0.0).astype(jnp.bfloat16)
 
         def step(group, carry):
-            direct = nt_dot(eye, spectra[0, group])
-            turn = nt_dot(eye, turned[group])
-            for q in range(BLK // TILE):
-                rows = slice(q * TILE, (q + 1) * TILE)
-                both = (
-                    direct[rows].reshape(TILE, 1, DEPTH) * direct_mask
-                    + turn[rows].reshape(TILE, 1, DEPTH) * turned_mask
-                )
-                expanded[group, q * TILE * 8 : (q + 1) * TILE * 8] = both.reshape(TILE * 8, DEPTH).astype(jnp.bfloat16)
+            sides[group] = nt_dot(eye, jnp.concatenate([spectra[0, group], turned[group]], axis=0))
             return carry
 
-        lax.fori_loop(0, GROUPS, step, 0, unroll=4)
-
-    def tile_lags(kind, tile):
+        lax.fori_loop(0, GROUPS, step, 0, unroll=8)
+
+    def tile_lags(step, kind, tile):
         row = lax.broadcasted_iota(jnp.int32, (DEPTH, BLK), 0)
-        first = jnp.where(row % 8 < 4, 1.0, 0.0).astype(jnp.bfloat16)
-        second = jnp.where(row % 8 < 4, 0.0, 1.0).astype(jnp.bfloat16)
-
-        left_rows = pl.ds(pl.multiple_of(dest(tile) * TILE * 8, TILE * 8), TILE * 8)
-
-        def gram_step(group, carry):
+        low_bins = jnp.where(row % 8 < 4, 1.0, 0.0).astype(jnp.bfloat16)
+        high_bins = jnp.where(row % 8 < 4, 0.0, 1.0).astype(jnp.bfloat16)
+        first = dest(tile) * TILE
+        left_rows = pl.ds(pl.multiple_of(first * 8, TILE * 8), TILE * 8)
+
+        def cross(group, left):
             right = spectra[kind, group]
-            weights = jnp.concatenate([right * first, right * second], axis=1)
-            cross = jnp.dot(expanded[group, left_rows], weights, preferred_element_type=jnp.float32)
-            cross = jnp.concatenate(
-                [cross[:, :BLK].reshape(TILE, 8, BLK), cross[:, BLK:].reshape(TILE, 8, BLK)], axis=1
+            weights = jnp.concatenate([right * low_bins, right * high_bins], axis=1)
+            both = jnp.dot(left, weights, preferred_element_type=jnp.float32)
+            both = jnp.concatenate(
+                [both[:, :BLK].reshape(TILE, 8, BLK), both[:, BLK:].reshape(TILE, 8, BLK)], axis=1
             )
             rows = pl.ds(pl.multiple_of(group * 16, 16), 16)
-            gram[:, rows, :] = cross.astype(jnp.bfloat16)
-            return carry
-
-        lax.fori_loop(0, GROUPS, gram_step, 0, unroll=16)
+            gram[:, rows, :] = both.astype(jnp.bfloat16)
+
+        @pl.when(step == 0)
+        def _():
+            row = lax.broadcasted_iota(jnp.int32, (8, DEPTH), 0)
+            col = lax.broadcasted_iota(jnp.int32, (8, DEPTH), 1)
+            mine = col % 4 == row // 2
+            direct_mask = jnp.where(mine & (row % 2 == 0), 1.0, 0.0)
+            turned_mask = jnp.where(mine & (row % 2 == 1), 1.0, 0.0)
+
+            def expand_step(group, carry):
+                parts = []
+                for i in range(TILE):
+                    line = sides[group, pl.ds(first + i, 1), :]
+                    parts.append(line[:, :DEPTH] * direct_mask + line[:, DEPTH:] * turned_mask)
+                left = jnp.concatenate(parts, axis=0).astype(jnp.bfloat16)
+                expanded[group, left_rows] = left
+                cross(group, left)
+                return carry
+
+            lax.fori_loop(0, GROUPS, expand_step, 0, unroll=4)
+
+        @pl.when(step > 0)
+        def _():
+            def gram_step(group, carry):
+                cross(group, expanded[group, left_rows])
+                return carry
+
+            lax.fori_loop(0, GROUPS, gram_step, 0, unroll=32)
 
         def lag_step(pair, carry):
             two = jnp.concatenate([gram[2 * pair], gram[2 * pair + 1]], axis=1)
@@ -279,15 +303,27 @@
                 from_down[kind, i].astype(jnp.float32) + from_up[kind, i].astype(jnp.float32)
             )
             drop = jnp.where(kind == 0, z * TILE + i, -1)
-            out_ref[kind, i] = jnp.where(column == drop, 0.0, total).astype(jnp.bfloat16)
+            done[kind, i] = jnp.where(column == drop, 0.0, total).astype(jnp.bfloat16)
             return carry
 
         lax.fori_loop(0, TILE, step, 0, unroll=4)
 
+        store(kind).start()
+
         @pl.when(kind == 2)
         def _():
             forward().start()
 
+    def match(p, slots):
+        apart = blocks_ref[p, 1] - blocks_ref[p, 0]
+        kind = jnp.where(blocks_ref[p, 0] == c, apart, 3)
+        owned = owner_ref[p] - c * SLOTS
+        return tuple(held + jnp.where(owned == q, kind + 1, 0) for q, held in enumerate(slots))
+
+    for q, held in enumerate(lax.fori_loop(0, owner_ref.shape[0], match, (0,) * SLOTS)):
+        kinds_ref[q] = held
+
+    table_copy.wait()
     own_halo.wait()
     whiten(own_ext, 0, True)
 
@@ -295,7 +331,7 @@
     def _():
         to_mate().start()
 
-    expand()
+    transpose()
 
     def kind_of(step):
         return lax.rem(step * (1 + odd), KINDS)
@@ -318,7 +354,7 @@
             to_mate().wait_recv()
 
         def tile_step(tile, carry):
-            tile_lags(kind, tile)
+            tile_lags(step, kind, tile)
             copies = sum_copies(kind)
 
             @pl.when(tile == OPP)
@@ -354,39 +390,51 @@
     for kind in range(KINDS):
         for copy in sum_copies(kind):
             copy.wait_send()
-    out_ref[3] = shared[...]
-
-
-def place_kernel(kinds_ref, live_ref, block_ref, out_ref):
-    q = pl.program_id(0)
-
-    @pl.when(live_ref[q] > 0)
-    def _():
-        out_ref[...] = block_ref[0]
-
-    @pl.when(live_ref[q] == 0)
-    def _():
-        out_ref[...] = jnp.zeros_like(out_ref)
+    for kind in range(KINDS):
+        store(kind).wait()
+
+
+def place_kernel(kinds_ref, stacks_ref, out_ref, zeros, sem):
+    zeros[...] = jnp.zeros_like(zeros)
+
+    def copy(q, src):
+        return pltpu.make_async_copy(src, out_ref.at[:, q], sem.at[q])
+
+    for q in range(SLOTS):
+        held = kinds_ref[q]
+
+        @pl.when(held > 0)
+        def _():
+            copy(q, stacks_ref.at[held - 1]).start()
+
+        @pl.when(held == 0)
+        def _():
+            copy(q, zeros).start()
+
+    for q in range(SLOTS):
+        copy(q, zeros).wait()
 
 
 def shards(n_chan, n_tm, record, seg_starts, pair_blocks, pair_owner):
     block_len = record.shape[1]
     scale = 2.0 / math.sqrt(SEGS_DEV * n_tm * F)
     bf16 = jnp.bfloat16
-    stacks = pl.pallas_call(
+    hbm = pl.BlockSpec(memory_space=pl.ANY)
+    smem = pl.BlockSpec(memory_space=pltpu.SMEM)
+    stacks, kinds = pl.pallas_call(
         functools.partial(stacks_kernel, n_chan, n_tm, scale),
-        out_shape=jax.ShapeDtypeStruct((4, TILE, NLAG, BLK), bf16),
-        in_specs=[
-            pl.BlockSpec(memory_space=pltpu.SMEM),
-            pl.BlockSpec(memory_space=pl.ANY),
-            pl.BlockSpec(memory_space=pltpu.VMEM),
-            pl.BlockSpec(memory_space=pltpu.VMEM),
-        ],
-        out_specs=pl.BlockSpec(memory_space=pltpu.VMEM),
+        out_shape=(
+            jax.ShapeDtypeStruct((4, TILE, NLAG, BLK), bf16),
+            jax.ShapeDtypeStruct((SLOTS,), jnp.int32),
+        ),
+        in_specs=[smem, smem, smem, hbm, hbm, pl.BlockSpec(memory_space=pltpu.VMEM)],
+        out_specs=(hbm, smem),
         scratch_shapes=[
+            pltpu.VMEM((2 * F, SEG_LEN), bf16),
             pltpu.VMEM(((block_len + SEG_LEN) // 128, BLK, 128), bf16),
             pltpu.VMEM(((block_len + SEG_LEN) // 128, BLK, 128), bf16),
             pltpu.VMEM((GROUPS, DEPTH, BLK), bf16),
+            pltpu.VMEM((GROUPS, BLK, 2 * DEPTH), jnp.float32),
             pltpu.VMEM((KINDS, GROUPS, DEPTH, BLK), bf16),
             pltpu.VMEM((GROUPS, BLK * 8, DEPTH), bf16),
             pltpu.VMEM((TILE, 2 * F, BLK), bf16),
@@ -395,8 +443,10 @@
             pltpu.VMEM((KINDS, HALF, NLAG, BLK), bf16),
             pltpu.VMEM((KINDS, TILE, NLAG, BLK), bf16),
             pltpu.VMEM((KINDS, TILE, NLAG, BLK), bf16),
-            pltpu.VMEM((TILE, NLAG, BLK), bf16),
+            pltpu.VMEM((KINDS, TILE, NLAG, BLK), bf16),
             pltpu.SemaphoreType.DMA((block_len // 128,)),
+            pltpu.SemaphoreType.DMA,
+            pltpu.SemaphoreType.DMA((KINDS,)),
             pltpu.SemaphoreType.DMA((5,)),
             pltpu.SemaphoreType.DMA((5,)),
             pltpu.SemaphoreType.DMA((KINDS, 6)),
@@ -406,26 +456,15 @@
             collective_id=0, has_side_effects=True, vmem_limit_bytes=60 * 1024 * 1024
         ),
         name="stacks",
-    )(seg_starts, record, transform_table(), lag_table())
-
-    chan = lax.axis_index("chan")
-    wanted = chan * SLOTS + jnp.arange(SLOTS, dtype=jnp.int32)
-    match = (pair_owner[None, :] == wanted[:, None]).astype(jnp.int32)
-    apart = pair_blocks[:, 1] - pair_blocks[:, 0]
-    kind = jnp.where((apart == 2) & (pair_blocks[:, 0] != chan), 3, apart)
-    live = jnp.sum(match, axis=1)
-    kinds = jnp.sum(match * kind[None, :], axis=1)
+    )(seg_starts, pair_blocks, pair_owner, record, transform_table(), lag_table())
     return pl.pallas_call(
         place_kernel,
         out_shape=jax.ShapeDtypeStruct((TILE, SLOTS, NLAG, BLK), bf16),
-        grid_spec=pltpu.PrefetchScalarGridSpec(
-            num_scalar_prefetch=2,
-            grid=(SLOTS,),
-            in_specs=[pl.BlockSpec((1, TILE, NLAG, BLK), lambda q, kinds, live: (kinds[q], 0, 0, 0))],
-            out_specs=pl.BlockSpec((TILE, None, NLAG, BLK), lambda q, kinds, live: (0, q, 0, 0)),
-        ),
+        in_specs=[smem, hbm],
+        out_specs=hbm,
+        scratch_shapes=[pltpu.VMEM((TILE, NLAG, BLK), bf16), pltpu.SemaphoreType.DMA((SLOTS,))],
         name="place",
-    )(kinds, live, stacks)
+    )(kinds, stacks)
 
 
 def solution(mesh):

time: 94 us -> 147 us (1.56)
  Pallas kernels: 91.5 us -> 146 us
  other arithmetic: 2.18 us -> 0 us
    pallas_call x1, Pallas kernels: 4.48 us -> 65.4 us  [shards(): pl.pallas_call(place_kernel, out_shape=jax.ShapeDtypeStruct((TILE, SLOTS,...]
    pallas_call x1, Pallas kernels: 87 us -> 80.4 us  [shards(): pl.pallas_call(functools.partial(stacks_kernel, n_chan, n_tm, scale), out...]
where the time goes in v3:
time: 147 us
  Pallas kernels  146 us (99%)
    pallas_call x1, Pallas kernels, shards(): pl.pallas_call(functools.partial(stacks_kernel, n_chan, n_tm, scale), out...  80.4 us
    pallas_call x1, Pallas kernels, shards(): pl.pallas_call(place_kernel, out_shape=jax.ShapeDtypeStruct((TILE, SLOTS,...  65.4 us

profile of v3, /device:TPU:1, one launch (start us, length us, event | category | flops | bytes accessed | tf_op | source)
XLA Modules:
  0.0 147.2 jit_solution(3549246507601705562)
XLA Ops:
  0.0 1.4 copy.7.blocks_ref
  1.4 80.4 %stacks.1 = (bf16[4,32,64,128]{3,2,1,0:T(8,128)(2,1)}, s32[4]{0:T(128)}) custom-call(s32[16]{0:T(128)} %starts_ref.1, s32[93,2]{1,0:T(8,128)} %copy.7.blocks_ref, s32[93]{0:T(128)} %owner_ref.1, bf16[128,4096]{1,0:T(8,128)(2,1)} %record_ref.1, bf16[512,512]{1,0:T(8,128)(2,1)} %constant.6.table_hbm, bf16[64,512]{1,0:T(8,128)(2,1)} %constant.7.lag_ref), custom_call_target="tpu_custom_call" | custom-call | tf_op jit(solution)/shard_map/stacks/pallas_call | solution.py:424
  81.8 65.4 %place.1 = bf16[32,4,64,128]{3,2,1,0:T(8,128)(2,1)} custom-call(s32[4]{0:T(128)} %get-tuple-element.7.kinds_ref, bf16[4,32,64,128]{3,2,1,0:T(8,128)(2,1)} %get-tuple-element.8.stacks_ref), custom_call_target="tpu_custom_call" | custom-call | tf_op jit(solution)/shard_map/place/pallas_call | solution.py:460

commit v4 on v3

--- a/solution.py
+++ b/solution.py
@@ -315,8 +315,8 @@
             forward().start()
 
     def match(p, slots):
-        apart = blocks_ref[p, 1] - blocks_ref[p, 0]
-        kind = jnp.where(blocks_ref[p, 0] == c, apart, 3)
+        apart = blocks_ref[1, p] - blocks_ref[0, p]
+        kind = jnp.where(blocks_ref[0, p] == c, apart, 3)
         owned = owner_ref[p] - c * SLOTS
         return tuple(held + jnp.where(owned == q, kind + 1, 0) for q, held in enumerate(slots))
 
@@ -394,25 +394,33 @@
         store(kind).wait()
 
 
-def place_kernel(kinds_ref, stacks_ref, out_ref, zeros, sem):
-    zeros[...] = jnp.zeros_like(zeros)
-
-    def copy(q, src):
-        return pltpu.make_async_copy(src, out_ref.at[:, q], sem.at[q])
+def place_kernel(kinds_ref, stacks_ref, out_ref, held, in_sem, out_sem):
+    def fetch(q):
+        return pltpu.make_async_copy(stacks_ref.at[kinds_ref[q] - 1], held.at[q], in_sem.at[q])
+
+    def put(q):
+        return pltpu.make_async_copy(held.at[q], out_ref.at[:, q], out_sem.at[q])
 
     for q in range(SLOTS):
-        held = kinds_ref[q]
-
-        @pl.when(held > 0)
-        def _():
-            copy(q, stacks_ref.at[held - 1]).start()
-
-        @pl.when(held == 0)
-        def _():
-            copy(q, zeros).start()
+
+        @pl.when(kinds_ref[q] > 0)
+        def _():
+            fetch(q).start()
+
+        @pl.when(kinds_ref[q] == 0)
+        def _():
+            held[q] = jnp.zeros_like(held[q])
 
     for q in range(SLOTS):
-        copy(q, zeros).wait()
+
+        @pl.when(kinds_ref[q] > 0)
+        def _():
+            fetch(q).wait()
+
+        put(q).start()
+
+    for q in range(SLOTS):
+        put(q).wait()
 
 
 def shards(n_chan, n_tm, record, seg_starts, pair_blocks, pair_owner):
@@ -456,13 +464,17 @@
             collective_id=0, has_side_effects=True, vmem_limit_bytes=60 * 1024 * 1024
         ),
         name="stacks",
-    )(seg_starts, pair_blocks, pair_owner, record, transform_table(), lag_table())
+    )(seg_starts, pair_blocks.T, pair_owner, record, transform_table(), lag_table())
     return pl.pallas_call(
         place_kernel,
         out_shape=jax.ShapeDtypeStruct((TILE, SLOTS, NLAG, BLK), bf16),
         in_specs=[smem, hbm],
         out_specs=hbm,
-        scratch_shapes=[pltpu.VMEM((TILE, NLAG, BLK), bf16), pltpu.SemaphoreType.DMA((SLOTS,))],
+        scratch_shapes=[
+            pltpu.VMEM((SLOTS, TILE, NLAG, BLK), bf16),
+            pltpu.SemaphoreType.DMA((SLOTS,)),
+            pltpu.SemaphoreType.DMA((SLOTS,)),
+        ],
         name="place",
     )(kinds, stacks)
 

time: 147 us -> 83.1 us (0.57)
  Pallas kernels: 146 us -> 82.9 us
    pallas_call x1, Pallas kernels: 65.4 us -> 3.09 us  [shards(): pl.pallas_call(place_kernel, out_shape=jax.ShapeDtypeStruct((TILE, SLOTS,...]
where the time goes in v4:
time: 83.1 us; the launch traced here: 82.9 us
  Pallas kernels  82.9 us (100%)
    pallas_call x1, Pallas kernels, shards(): pl.pallas_call(functools.partial(stacks_kernel, n_chan, n_tm, scale), out...  79.8 us
    pallas_call x1, Pallas kernels, shards(): pl.pallas_call(place_kernel, out_shape=jax.ShapeDtypeStruct((TILE, SLOTS,...  3.09 us

profile of v4, /device:TPU:1, one launch (start us, length us, event | category | flops | bytes accessed | tf_op | source)
XLA Modules:
  0.0 82.9 jit_solution(18274244564990728057)
XLA Ops:
  0.0 79.8 %stacks.1 = (bf16[4,32,64,128]{3,2,1,0:T(8,128)(2,1)}, s32[4]{0:T(128)}) custom-call(s32[16]{0:T(128)} %starts_ref.1, s32[2,93]{1,0:T(2,128)} %bitcast.1, s32[93]{0:T(128)} %owner_ref.1, bf16[128,4096]{1,0:T(8,128)(2,1)} %record_ref.1, bf16[512,512]{1,0:T(8,128)(2,1)} %constant.6.table_hbm, bf16[64,512]{1,0:T(8,128)(2,1)} %constant.7.lag_ref), custom_call_target="tpu_custom_call" | custom-call | tf_op jit(solution)/shard_map/stacks/pallas_call | solution.py:432
  79.8 3.1 %place.1 = bf16[32,4,64,128]{3,2,1,0:T(8,128)(2,1)} custom-call(s32[4]{0:T(128)} %get-tuple-element.7.kinds_ref, bf16[4,32,64,128]{3,2,1,0:T(8,128)(2,1)} %get-tuple-element.8.stacks_ref), custom_call_target="tpu_custom_call" | custom-call | tf_op jit(solution)/shard_map/place/pallas_call | solution.py:468

commit v5 on v3

--- a/solution.py
+++ b/solution.py
@@ -75,10 +75,9 @@
     relay_down,
     from_down,
     from_up,
-    done,
+    shared,
     local_sem,
     table_sem,
-    done_sem,
     near_send,
     near_recv,
     sum_send,
@@ -115,9 +114,9 @@
     table_copy.start()
 
     barrier = pltpu.get_barrier_semaphore()
-    for who in ((c, up), (c, down), (c_next2, z), (c_next2, up), (mate, z), (c_prev, z)):
+    for who in ((c, up), (c, down), (c_next2, z), (mate, z), (c_prev, z)):
         pl.semaphore_signal(barrier, inc=1, device_id=who, device_id_type=MESH)
-    pl.semaphore_wait(barrier, 6)
+    pl.semaphore_wait(barrier, 5)
 
     def near(index, src, dst, who):
         return pltpu.make_async_remote_copy(
@@ -132,21 +131,17 @@
     main, halo = pl.ds(0, tiles), pl.ds(tiles, SEG_LEN // 128)
     head = own_ext.at[pl.ds(0, SEG_LEN // 128)]
     own_halo = near(0, head, own_ext.at[halo], (c, down))
-    next_halo = near(1, head, next_ext.at[halo], (c_prev2, down))
+    next_halo = near(1, own_ext.at[halo], next_ext.at[halo], (c_prev2, z))
     next_main = near(2, own_ext.at[main], next_ext.at[main], (c_prev2, z))
     lax.fori_loop(0, tiles, wait_load, 0)
     own_halo.start()
-    next_halo.start()
     next_main.start()
 
     def to_mate():
         return near(3, spectra.at[2 - 2 * odd], spectra.at[1], (mate, z))
 
     def forward():
-        return near(4, done.at[2], out_ref.at[3], (c_next, z))
-
-    def store(kind):
-        return pltpu.make_async_copy(done.at[kind], out_ref.at[kind], done_sem.at[kind])
+        return near(4, out_ref.at[2], shared, (c_next, z))
 
     def sum_copies(kind):
         low, high = pl.ds(0, HALF), pl.ds(HALF, HALF)
@@ -239,18 +234,19 @@
 
         @pl.when(step == 0)
         def _():
-            row = lax.broadcasted_iota(jnp.int32, (8, DEPTH), 0)
-            col = lax.broadcasted_iota(jnp.int32, (8, DEPTH), 1)
-            mine = col % 4 == row // 2
-            direct_mask = jnp.where(mine & (row % 2 == 0), 1.0, 0.0)
-            turned_mask = jnp.where(mine & (row % 2 == 1), 1.0, 0.0)
+            direct_row = lax.broadcasted_iota(jnp.int32, (8, DEPTH), 0) % 2 == 0
+            row = lax.broadcasted_iota(jnp.int32, (16, DEPTH), 0)
+            col = lax.broadcasted_iota(jnp.int32, (16, DEPTH), 1)
+            mine = jnp.where(col % 4 == (row // 2) % 4, 1.0, 0.0).astype(jnp.bfloat16)
 
             def expand_step(group, carry):
                 parts = []
-                for i in range(TILE):
-                    line = sides[group, pl.ds(first + i, 1), :]
-                    parts.append(line[:, :DEPTH] * direct_mask + line[:, DEPTH:] * turned_mask)
-                left = jnp.concatenate(parts, axis=0).astype(jnp.bfloat16)
+                for i in range(0, TILE, 2):
+                    two = []
+                    for line in (sides[group, pl.ds(first + i, 1), :], sides[group, pl.ds(first + i + 1, 1), :]):
+                        two.append(jnp.where(direct_row, line[:, :DEPTH], line[:, DEPTH:]))
+                    parts.append(jnp.concatenate(two, axis=0).astype(jnp.bfloat16) * mine)
+                left = jnp.concatenate(parts, axis=0)
                 expanded[group, left_rows] = left
                 cross(group, left)
                 return carry
@@ -272,7 +268,19 @@
             part[kind, tile, 2 * pair + 1] = lags[:, BLK:].astype(jnp.bfloat16)
             return carry
 
-        lax.fori_loop(0, TILE // 2, lag_step, 0, unroll=16)
+        copies = sum_copies(kind)
+
+        def half(h, carry):
+            lax.fori_loop(0, HALF // 2, lambda i, carry: lag_step(h * (HALF // 2) + i, carry), 0, unroll=8)
+            for index, (of_tile, of_half) in ((0, (OPP, 0)), (1, (OPP, 1)), (2, (UP, 1)), (4, (DOWN, 0))):
+
+                @pl.when((tile == of_tile) & (h == of_half))
+                def _():
+                    copies[index].start()
+
+            return carry
+
+        lax.fori_loop(0, 2, half, 0)
 
     def relay(kind):
         copies = sum_copies(kind)
@@ -303,20 +311,18 @@
                 from_down[kind, i].astype(jnp.float32) + from_up[kind, i].astype(jnp.float32)
             )
             drop = jnp.where(kind == 0, z * TILE + i, -1)
-            done[kind, i] = jnp.where(column == drop, 0.0, total).astype(jnp.bfloat16)
+            out_ref[kind, i] = jnp.where(column == drop, 0.0, total).astype(jnp.bfloat16)
             return carry
 
         lax.fori_loop(0, TILE, step, 0, unroll=4)
 
-        store(kind).start()
-
         @pl.when(kind == 2)
         def _():
             forward().start()
 
     def match(p, slots):
-        apart = blocks_ref[p, 1] - blocks_ref[p, 0]
-        kind = jnp.where(blocks_ref[p, 0] == c, apart, 3)
+        apart = blocks_ref[1, p] - blocks_ref[0, p]
+        kind = jnp.where(blocks_ref[0, p] == c, apart, 3)
         owned = owner_ref[p] - c * SLOTS
         return tuple(held + jnp.where(owned == q, kind + 1, 0) for q, held in enumerate(slots))
 
@@ -325,6 +331,7 @@
 
     table_copy.wait()
     own_halo.wait()
+    next_halo.start()
     whiten(own_ext, 0, True)
 
     @pl.when(odd == 1)
@@ -355,21 +362,6 @@
 
         def tile_step(tile, carry):
             tile_lags(step, kind, tile)
-            copies = sum_copies(kind)
-
-            @pl.when(tile == OPP)
-            def _():
-                copies[0].start()
-                copies[1].start()
-
-            @pl.when(tile == UP)
-            def _():
-                copies[2].start()
-
-            @pl.when(tile == DOWN)
-            def _():
-                copies[4].start()
-
             return carry
 
         lax.fori_loop(0, 4, tile_step, 0)
@@ -390,14 +382,13 @@
     for kind in range(KINDS):
         for copy in sum_copies(kind):
             copy.wait_send()
-    for kind in range(KINDS):
-        store(kind).wait()
+    out_ref[3] = shared[...]
 
 
 def place_kernel(kinds_ref, stacks_ref, out_ref, zeros, sem):
     zeros[...] = jnp.zeros_like(zeros)
 
-    def copy(q, src):
+    def put(q, src):
         return pltpu.make_async_copy(src, out_ref.at[:, q], sem.at[q])
 
     for q in range(SLOTS):
@@ -405,14 +396,14 @@
 
         @pl.when(held > 0)
         def _():
-            copy(q, stacks_ref.at[held - 1]).start()
+            put(q, stacks_ref.at[held - 1]).start()
 
         @pl.when(held == 0)
         def _():
-            copy(q, zeros).start()
+            put(q, zeros).start()
 
     for q in range(SLOTS):
-        copy(q, zeros).wait()
+        put(q, zeros).wait()
 
 
 def shards(n_chan, n_tm, record, seg_starts, pair_blocks, pair_owner):
@@ -421,14 +412,15 @@
     bf16 = jnp.bfloat16
     hbm = pl.BlockSpec(memory_space=pl.ANY)
     smem = pl.BlockSpec(memory_space=pltpu.SMEM)
+    vmem = pl.BlockSpec(memory_space=pltpu.VMEM)
     stacks, kinds = pl.pallas_call(
         functools.partial(stacks_kernel, n_chan, n_tm, scale),
         out_shape=(
-            jax.ShapeDtypeStruct((4, TILE, NLAG, BLK), bf16),
+            pltpu.VMEM((4, TILE, NLAG, BLK), bf16),
             jax.ShapeDtypeStruct((SLOTS,), jnp.int32),
         ),
-        in_specs=[smem, smem, smem, hbm, hbm, pl.BlockSpec(memory_space=pltpu.VMEM)],
-        out_specs=(hbm, smem),
+        in_specs=[smem, smem, smem, hbm, hbm, vmem],
+        out_specs=(vmem, smem),
         scratch_shapes=[
             pltpu.VMEM((2 * F, SEG_LEN), bf16),
             pltpu.VMEM(((block_len + SEG_LEN) // 128, BLK, 128), bf16),
@@ -443,10 +435,9 @@
             pltpu.VMEM((KINDS, HALF, NLAG, BLK), bf16),
             pltpu.VMEM((KINDS, TILE, NLAG, BLK), bf16),
             pltpu.VMEM((KINDS, TILE, NLAG, BLK), bf16),
-            pltpu.VMEM((KINDS, TILE, NLAG, BLK), bf16),
+            pltpu.VMEM((TILE, NLAG, BLK), bf16),
             pltpu.SemaphoreType.DMA((block_len // 128,)),
             pltpu.SemaphoreType.DMA,
-            pltpu.SemaphoreType.DMA((KINDS,)),
             pltpu.SemaphoreType.DMA((5,)),
             pltpu.SemaphoreType.DMA((5,)),
             pltpu.SemaphoreType.DMA((KINDS, 6)),
@@ -456,11 +447,11 @@
             collective_id=0, has_side_effects=True, vmem_limit_bytes=60 * 1024 * 1024
         ),
         name="stacks",
-    )(seg_starts, pair_blocks, pair_owner, record, transform_table(), lag_table())
+    )(seg_starts, pair_blocks.T, pair_owner, record, transform_table(), lag_table())
     return pl.pallas_call(
         place_kernel,
         out_shape=jax.ShapeDtypeStruct((TILE, SLOTS, NLAG, BLK), bf16),
-        in_specs=[smem, hbm],
+        in_specs=[smem, vmem],
         out_specs=hbm,
         scratch_shapes=[pltpu.VMEM((TILE, NLAG, BLK), bf16), pltpu.SemaphoreType.DMA((SLOTS,))],
         name="place",

time: 147 us -> 81.7 us (0.56)
  Pallas kernels: 146 us -> 79.6 us
    pallas_call x1, Pallas kernels: 65.4 us -> 2.95 us  [shards(): pl.pallas_call(place_kernel, out_shape=jax.ShapeDtypeStruct((TILE, SLOTS,...]
    pallas_call x1, Pallas kernels: 80.4 us -> 76.6 us  [shards(): pl.pallas_call(functools.partial(stacks_kernel, n_chan, n_tm, scale), out...]
where the time goes in v5:
time: 81.7 us; the launch traced here: 80.9 us
  Pallas kernels  79.6 us (97%)
  local copies, waits for them, and re-layouts  1.33 us (2%)
    pallas_call x1, Pallas kernels, shards(): pl.pallas_call(functools.partial(stacks_kernel, n_chan, n_tm, scale), out...  76.6 us
    pallas_call x1, Pallas kernels, shards(): pl.pallas_call(place_kernel, out_shape=jax.ShapeDtypeStruct((TILE, SLOTS,...  2.95 us

profile of v5, /device:TPU:1, one launch (start us, length us, event | category | flops | bytes accessed | tf_op | source)
XLA Modules:
  0.0 80.9 jit_solution(3861422593502783533)
XLA Ops:
  0.0 76.6 %stacks.1 = (bf16[4,32,64,128]{3,2,1,0:T(8,128)(2,1)S(1)}, s32[4]{0:T(128)}) custom-call(s32[16]{0:T(128)} %starts_ref.1, s32[2,93]{1,0:T(2,128)} %bitcast.1, s32[93]{0:T(128)} %owner_ref.1, bf16[128,4096]{1,0:T(8,128)(2,1)} %record_ref.1, bf16[512,512]{1,0:T(8,128)(2,1)} %constant.6.table_hbm, bf16[64,512]{1,0:T(8,128)(2,1)} %constant.7.lag_ref), custom_call_target="tpu_custom_call" | custom-call | tf_op jit(solution)/shard_map/stacks/pallas_call | solution.py:416
  76.7 0.0 copy-start
  76.7 1.3 %copy-done = bf16[4,32,64,128]{3,2,1,0:T(8,128)(2,1)} copy-done((bf16[4,32,64,128]{3,2,1,0:T(8,128)(2,1)}, bf16[4,32,64,128]{3,2,1,0:T(8,128)(2,1)S(1)}, u32[]{:S(2)}) %copy-start) | copy-done | bytes 2097176
  78.0 2.9 %place.1 = bf16[32,4,64,128]{3,2,1,0:T(8,128)(2,1)} custom-call(s32[4]{0:T(128)} %get-tuple-element.7.kinds_ref, bf16[4,32,64,128]{3,2,1,0:T(8,128)(2,1)} %copy-done), custom_call_target="tpu_custom_call" | custom-call | tf_op jit(solution)/shard_map/place/pallas_call | solution.py:451
Async XLA Ops:
  76.7 1.3 %copy-start = (bf16[4,32,64,128]{3,2,1,0:T(8,128)(2,1)}, bf16[4,32,64,128]{3,2,1,0:T(8,128)(2,1)S(1)}, u32[]{:S(2)}) copy-start(bf16[4,32,64,128]{3,2,1,0:T(8,128)(2,1)S(1)} %get-tuple-element.8.stacks_ref) | copy-start | bytes 6291460

commit v6 on v5

--- a/solution.py
+++ b/solution.py
@@ -327,7 +327,7 @@
         return tuple(held + jnp.where(owned == q, kind + 1, 0) for q, held in enumerate(slots))
 
     for q, held in enumerate(lax.fori_loop(0, owner_ref.shape[0], match, (0,) * SLOTS)):
-        kinds_ref[q] = held
+        kinds_ref[q] = jnp.minimum(held, KINDS + 1)
 
     table_copy.wait()
     own_halo.wait()
@@ -417,7 +417,7 @@
         functools.partial(stacks_kernel, n_chan, n_tm, scale),
         out_shape=(
             pltpu.VMEM((4, TILE, NLAG, BLK), bf16),
-            jax.ShapeDtypeStruct((SLOTS,), jnp.int32),
+            pltpu.SMEM((SLOTS,), jnp.int32),
         ),
         in_specs=[smem, smem, smem, hbm, hbm, vmem],
         out_specs=(vmem, smem),
@@ -454,8 +454,9 @@
         in_specs=[smem, vmem],
         out_specs=hbm,
         scratch_shapes=[pltpu.VMEM((TILE, NLAG, BLK), bf16), pltpu.SemaphoreType.DMA((SLOTS,))],
+        compiler_params=pltpu.CompilerParams(vmem_limit_bytes=4 * 1024 * 1024),
         name="place",
-    )(kinds, stacks)
+    )(kinds, pltpu.with_memory_space_constraint(stacks, pltpu.VMEM))
 
 
 def solution(mesh):

time: 81.7 us -> 78.3 us (0.958)
  Pallas kernels: 79.6 us -> 77.5 us
  local copies, waits for them, and re-layouts: 1.33 us -> 0 us
    pallas_call x1, Pallas kernels: 2.95 us -> 1.35 us  [shards(): pl.pallas_call(place_kernel, out_shape=jax.ShapeDtypeStruct((TILE, SLOTS,...]
    unnamed x2 -> x0, local copies, waits for them, and re-layouts: 1.33 us -> none
where the time goes in v6:
time: 78.3 us; the launch traced here: 77.5 us
  Pallas kernels  77.5 us (99%)
    pallas_call x1, Pallas kernels, shards(): pl.pallas_call(functools.partial(stacks_kernel, n_chan, n_tm, scale), out...  76.2 us

profile of v6, /device:TPU:1, one launch (start us, length us, event | category | flops | bytes accessed | tf_op | source)
XLA Modules:
  0.0 77.5 jit_solution(1977498007964293141)
XLA Ops:
  0.0 76.2 %stacks.1 = (bf16[4,32,64,128]{3,2,1,0:T(8,128)(2,1)S(1)}, s32[4]{0:T(128)S(4)}) custom-call(s32[16]{0:T(128)} %starts_ref.1, s32[2,93]{1,0:T(2,128)} %bitcast.1, s32[93]{0:T(128)} %owner_ref.1, bf16[128,4096]{1,0:T(8,128)(2,1)} %record_ref.1, bf16[512,512]{1,0:T(8,128)(2,1)} %constant.6.table_hbm, bf16[64,512]{1,0:T(8,128)(2,1)} %constant.7.lag_ref), custom_call_target="tpu_custom_call" | custom-call | tf_op jit(solution)/shard_map/stacks/pallas_call | solution.py:416
  76.2 1.4 %place.1 = bf16[32,4,64,128]{3,2,1,0:T(8,128)(2,1)} custom-call(s32[4]{0:T(128)S(4)} %get-tuple-element.7.kinds_ref, bf16[4,32,64,128]{3,2,1,0:T(8,128)(2,1)S(1)} %get-tuple-element.8.stacks_ref), custom_call_target="tpu_custom_call" | custom-call | tf_op jit(solution)/shard_map/place/pallas_call | solution.py:451

commit v7 on v6

--- a/solution.py
+++ b/solution.py
@@ -27,6 +27,7 @@
 HALF = TILE // 2
 KINDS = 3
 OPP, UP, DOWN, OWN = range(4)
+MIRROR = NLAG // 2
 
 
 def transform_table():
@@ -38,11 +39,10 @@
     return jnp.asarray(table.astype(np.float32)).astype(jnp.bfloat16)
 
 
-def lag_table():
-    shifts = np.arange(NLAG) - NLAG // 2
+def lag_table(shifts):
     bins = np.arange(F) + LOW_BIN
     phase = (bins[:, None] * shifts[None, :] % SEG_LEN) * (2.0 * math.pi / SEG_LEN)
-    table = np.stack([np.cos(phase), -np.sin(phase)], axis=1).reshape(2 * F, NLAG)
+    table = np.stack([np.cos(phase), -np.sin(phase)], axis=1).reshape(2 * F, len(shifts))
     return jnp.asarray(np.ascontiguousarray(table.T).astype(np.float32)).astype(jnp.bfloat16)
 
 
@@ -60,6 +60,7 @@
     record_ref,
     table_hbm,
     lag_ref,
+    self_lag_ref,
     out_ref,
     kinds_ref,
     table_ref,
@@ -75,6 +76,16 @@
     relay_down,
     from_down,
     from_up,
+    self_part,
+    self_relay_up,
+    self_relay_down,
+    self_from_down,
+    self_from_up,
+    zero_lag,
+    folded,
+    unfolded,
+    mirror_out,
+    mirror_in,
     shared,
     local_sem,
     table_sem,
@@ -82,12 +93,15 @@
     near_recv,
     sum_send,
     sum_recv,
+    mirror_send,
+    mirror_recv,
 ):
     c = lax.axis_index("chan")
     z = lax.axis_index("tm")
     block_len = record_ref.shape[1]
     up = lax.rem(z + 1, n_tm)
     down = lax.rem(z + n_tm - 1, n_tm)
+    opposite = lax.rem(z + 2, n_tm)
     c_next = lax.rem(c + 1, n_chan)
     c_prev = lax.rem(c + n_chan - 1, n_chan)
     c_next2 = lax.rem(c + 2, n_chan)
@@ -114,9 +128,9 @@
     table_copy.start()
 
     barrier = pltpu.get_barrier_semaphore()
-    for who in ((c, up), (c, down), (c_next2, z), (mate, z), (c_prev, z)):
+    for who in ((c, up), (c, down), (c, opposite), (c_next2, z), (mate, z), (c_prev, z)):
         pl.semaphore_signal(barrier, inc=1, device_id=who, device_id_type=MESH)
-    pl.semaphore_wait(barrier, 5)
+    pl.semaphore_wait(barrier, 6)
 
     def near(index, src, dst, who):
         return pltpu.make_async_remote_copy(
@@ -143,15 +157,14 @@
     def forward():
         return near(4, out_ref.at[2], shared, (c_next, z))
 
-    def sum_copies(kind):
-        low, high = pl.ds(0, HALF), pl.ds(HALF, HALF)
+    def ring_copies(kind, piece, up_slot, down_slot, below, above):
         routes = (
-            (part.at[kind, OPP, low], relay_up.at[kind], up),
-            (part.at[kind, OPP, high], relay_down.at[kind], down),
-            (part.at[kind, UP, high], from_down.at[kind, high], up),
-            (part.at[kind, UP, low], from_down.at[kind, low], up),
-            (part.at[kind, DOWN, low], from_up.at[kind, low], down),
-            (part.at[kind, DOWN, high], from_up.at[kind, high], down),
+            (piece(OPP, 0), up_slot, up),
+            (piece(OPP, 1), down_slot, down),
+            (piece(UP, 1), below(1), up),
+            (piece(UP, 0), below(0), up),
+            (piece(DOWN, 0), above(0), down),
+            (piece(DOWN, 1), above(1), down),
         )
         return [
             pltpu.make_async_remote_copy(
@@ -163,6 +176,43 @@
                 device_id_type=MESH,
             )
             for index, (src, dst, who) in enumerate(routes)
+        ]
+
+    def sum_copies(kind):
+        def rows(half):
+            return pl.ds(half * HALF, HALF)
+
+        k = kind - 1
+        return ring_copies(
+            kind,
+            lambda tile, half: part.at[k, tile, rows(half)],
+            relay_up.at[k],
+            relay_down.at[k],
+            lambda half: from_down.at[k, rows(half)],
+            lambda half: from_up.at[k, rows(half)],
+        )
+
+    def self_copies():
+        return ring_copies(
+            0,
+            lambda tile, half: self_part.at[tile, half],
+            self_relay_up,
+            self_relay_down,
+            lambda half: self_from_down.at[half],
+            lambda half: self_from_up.at[half],
+        )
+
+    def mirror_copies():
+        return [
+            pltpu.make_async_remote_copy(
+                src_ref=mirror_out.at[who],
+                dst_ref=mirror_in.at[index],
+                send_sem=mirror_send.at[index],
+                recv_sem=mirror_recv.at[index],
+                device_id=(c, who),
+                device_id_type=MESH,
+            )
+            for index, who in enumerate((opposite, up, down))
         ]
 
     lane = lax.broadcasted_iota(jnp.int32, (BLK, 128), 1)
@@ -215,103 +265,129 @@
 
         lax.fori_loop(0, GROUPS, step, 0, unroll=8)
 
-    def tile_lags(step, kind, tile):
+    def cross(kind, group, left):
         row = lax.broadcasted_iota(jnp.int32, (DEPTH, BLK), 0)
         low_bins = jnp.where(row % 8 < 4, 1.0, 0.0).astype(jnp.bfloat16)
         high_bins = jnp.where(row % 8 < 4, 0.0, 1.0).astype(jnp.bfloat16)
+        right = spectra[kind, group]
+        weights = jnp.concatenate([right * low_bins, right * high_bins], axis=1)
+        both = jnp.dot(left, weights, preferred_element_type=jnp.float32)
+        both = jnp.concatenate(
+            [both[:, :BLK].reshape(TILE, 8, BLK), both[:, BLK:].reshape(TILE, 8, BLK)], axis=1
+        )
+        rows = pl.ds(pl.multiple_of(group * 16, 16), 16)
+        gram[:, rows, :] = both.astype(jnp.bfloat16)
+
+    def left_rows(tile):
+        return pl.ds(pl.multiple_of(dest(tile) * TILE * 8, TILE * 8), TILE * 8)
+
+    def pair_lags(table, pair):
+        two = jnp.concatenate([gram[2 * pair], gram[2 * pair + 1]], axis=1)
+        lags = jnp.dot(table, two, preferred_element_type=jnp.float32) * scale
+        return lags[:, :BLK], lags[:, BLK:]
+
+    def start_ready(copies, tile, h):
+        for index, (of_tile, of_half) in ((0, (OPP, 0)), (1, (OPP, 1)), (2, (UP, 1)), (4, (DOWN, 0))):
+
+            @pl.when((tile == of_tile) & (h == of_half))
+            def _():
+                copies[index].start()
+
+    def self_tile(tile):
+        direct_row = lax.broadcasted_iota(jnp.int32, (8, DEPTH), 0) % 2 == 0
+        row = lax.broadcasted_iota(jnp.int32, (16, DEPTH), 0)
+        col = lax.broadcasted_iota(jnp.int32, (16, DEPTH), 1)
+        mine = jnp.where(col % 4 == (row // 2) % 4, 1.0, 0.0).astype(jnp.bfloat16)
         first = dest(tile) * TILE
-        left_rows = pl.ds(pl.multiple_of(first * 8, TILE * 8), TILE * 8)
-
-        def cross(group, left):
-            right = spectra[kind, group]
-            weights = jnp.concatenate([right * low_bins, right * high_bins], axis=1)
-            both = jnp.dot(left, weights, preferred_element_type=jnp.float32)
-            both = jnp.concatenate(
-                [both[:, :BLK].reshape(TILE, 8, BLK), both[:, BLK:].reshape(TILE, 8, BLK)], axis=1
-            )
-            rows = pl.ds(pl.multiple_of(group * 16, 16), 16)
-            gram[:, rows, :] = both.astype(jnp.bfloat16)
-
-        @pl.when(step == 0)
-        def _():
-            direct_row = lax.broadcasted_iota(jnp.int32, (8, DEPTH), 0) % 2 == 0
-            row = lax.broadcasted_iota(jnp.int32, (16, DEPTH), 0)
-            col = lax.broadcasted_iota(jnp.int32, (16, DEPTH), 1)
-            mine = jnp.where(col % 4 == (row // 2) % 4, 1.0, 0.0).astype(jnp.bfloat16)
-
-            def expand_step(group, carry):
-                parts = []
-                for i in range(0, TILE, 2):
-                    two = []
-                    for line in (sides[group, pl.ds(first + i, 1), :], sides[group, pl.ds(first + i + 1, 1), :]):
-                        two.append(jnp.where(direct_row, line[:, :DEPTH], line[:, DEPTH:]))
-                    parts.append(jnp.concatenate(two, axis=0).astype(jnp.bfloat16) * mine)
-                left = jnp.concatenate(parts, axis=0)
-                expanded[group, left_rows] = left
-                cross(group, left)
+
+        def expand_step(group, carry):
+            parts = []
+            for i in range(0, TILE, 2):
+                two = []
+                for line in (sides[group, pl.ds(first + i, 1), :], sides[group, pl.ds(first + i + 1, 1), :]):
+                    two.append(jnp.where(direct_row, line[:, :DEPTH], line[:, DEPTH:]))
+                parts.append(jnp.concatenate(two, axis=0).astype(jnp.bfloat16) * mine)
+            left = jnp.concatenate(parts, axis=0)
+            expanded[group, left_rows(tile)] = left
+            cross(0, group, left)
+            return carry
+
+        lax.fori_loop(0, GROUPS, expand_step, 0, unroll=4)
+        copies = self_copies()
+
+        def half(h, carry):
+            def lag_step(i, carry):
+                for k, lags in enumerate(pair_lags(self_lag_ref[...], h * (HALF // 2) + i)):
+                    self_part[tile, h, 2 * i + k] = lags[:MIRROR].astype(jnp.bfloat16)
+                    zero_lag[pl.ds(2 * i + k, 1), :] = lags[MIRROR : MIRROR + 1]
                 return carry
 
-            lax.fori_loop(0, GROUPS, expand_step, 0, unroll=4)
-
-        @pl.when(step > 0)
-        def _():
-            def gram_step(group, carry):
-                cross(group, expanded[group, left_rows])
+            lax.fori_loop(0, HALF // 2, lag_step, 0, unroll=8)
+            self_part[tile, h, HALF] = zero_lag[...].astype(jnp.bfloat16)
+            start_ready(copies, tile, h)
+            return carry
+
+        lax.fori_loop(0, 2, half, 0)
+
+    def kind_tile(kind, tile):
+        def gram_step(group, carry):
+            cross(kind, group, expanded[group, left_rows(tile)])
+            return carry
+
+        lax.fori_loop(0, GROUPS, gram_step, 0, unroll=32)
+        copies = sum_copies(kind)
+
+        def half(h, carry):
+            def lag_step(i, carry):
+                pair = h * (HALF // 2) + i
+                for k, lags in enumerate(pair_lags(lag_ref[...], pair)):
+                    part[kind - 1, tile, 2 * pair + k] = lags.astype(jnp.bfloat16)
                 return carry
 
-            lax.fori_loop(0, GROUPS, gram_step, 0, unroll=32)
-
-        def lag_step(pair, carry):
-            two = jnp.concatenate([gram[2 * pair], gram[2 * pair + 1]], axis=1)
-            lags = jnp.dot(lag_ref[...], two, preferred_element_type=jnp.float32) * scale
-            part[kind, tile, 2 * pair] = lags[:, :BLK].astype(jnp.bfloat16)
-            part[kind, tile, 2 * pair + 1] = lags[:, BLK:].astype(jnp.bfloat16)
-            return carry
-
-        copies = sum_copies(kind)
-
-        def half(h, carry):
-            lax.fori_loop(0, HALF // 2, lambda i, carry: lag_step(h * (HALF // 2) + i, carry), 0, unroll=8)
-            for index, (of_tile, of_half) in ((0, (OPP, 0)), (1, (OPP, 1)), (2, (UP, 1)), (4, (DOWN, 0))):
-
-                @pl.when((tile == of_tile) & (h == of_half))
-                def _():
-                    copies[index].start()
-
+            lax.fori_loop(0, HALF // 2, lag_step, 0, unroll=8)
+            start_ready(copies, tile, h)
             return carry
 
         lax.fori_loop(0, 2, half, 0)
+
+    def add(count, total, rows, held, held_rows):
+        def step(i, carry):
+            here = rows(i)
+            total[here] = (total[here].astype(jnp.float32) + held[held_rows(i)].astype(jnp.float32)).astype(jnp.bfloat16)
+            return carry
+
+        lax.fori_loop(0, count, step, 0, unroll=4 if count % 4 == 0 else 1)
 
     def relay(kind):
         copies = sum_copies(kind)
-
-        def add(tile, first_row, held):
-            def step(i, carry):
-                total = part[kind, tile, first_row + i].astype(jnp.float32) + held[kind, i].astype(jnp.float32)
-                part[kind, tile, first_row + i] = total.astype(jnp.bfloat16)
-                return carry
-
-            lax.fori_loop(0, HALF, step, 0, unroll=4)
-
+        k = kind - 1
         copies[0].wait_recv()
-        add(UP, 0, relay_up)
+        add(HALF, part, lambda i: (k, UP, i), relay_up, lambda i: (k, i))
         copies[3].start()
         copies[1].wait_recv()
-        add(DOWN, HALF, relay_down)
+        add(HALF, part, lambda i: (k, DOWN, HALF + i), relay_down, lambda i: (k, i))
         copies[5].start()
+
+    def self_relay():
+        copies = self_copies()
+        copies[0].wait_recv()
+        add(HALF + 1, self_part, lambda i: (UP, 0, i), self_relay_up, lambda i: i)
+        copies[3].start()
+        copies[1].wait_recv()
+        add(HALF + 1, self_part, lambda i: (DOWN, 1, i), self_relay_down, lambda i: i)
+        copies[5].start()
+
+    def three(own, below, above):
+        return own.astype(jnp.float32) + (below.astype(jnp.float32) + above.astype(jnp.float32))
 
     def finish(kind):
         copies = sum_copies(kind)
         for index in (2, 3, 4, 5):
             copies[index].wait_recv()
-        column = lax.broadcasted_iota(jnp.int32, (NLAG, BLK), 1)
+        k = kind - 1
 
         def step(i, carry):
-            total = part[kind, OWN, i].astype(jnp.float32) + (
-                from_down[kind, i].astype(jnp.float32) + from_up[kind, i].astype(jnp.float32)
-            )
-            drop = jnp.where(kind == 0, z * TILE + i, -1)
-            out_ref[kind, i] = jnp.where(column == drop, 0.0, total).astype(jnp.bfloat16)
+            out_ref[kind, i] = three(part[k, OWN, i], from_down[k, i], from_up[k, i]).astype(jnp.bfloat16)
             return carry
 
         lax.fori_loop(0, TILE, step, 0, unroll=4)
@@ -319,6 +395,62 @@
         @pl.when(kind == 2)
         def _():
             forward().start()
+
+    def self_finish():
+        copies = self_copies()
+        for index in (2, 3, 4, 5):
+            copies[index].wait_recv()
+        column = lax.broadcasted_iota(jnp.int32, (MIRROR, BLK), 1)
+        row = lax.broadcasted_iota(jnp.int32, (MIRROR, BLK), 0)
+
+        def half(h, carry):
+            zero_lag[...] = three(self_part[OWN, h, HALF], self_from_down[h, HALF], self_from_up[h, HALF])
+
+            def step(i, carry):
+                total = three(self_part[OWN, h, i], self_from_down[h, i], self_from_up[h, i])
+                mine = h * HALF + i
+                total = jnp.where(column == z * TILE + mine, 0.0, total)
+                folded[pl.ds(pl.multiple_of(mine * MIRROR, MIRROR), MIRROR), :] = total
+                zero = jnp.where(column == z * TILE + mine, 0.0, zero_lag[pl.ds(i, 1), :])
+                later = jnp.where(row == 0, zero, pltpu.roll(total, 1, 0))
+                out_ref[0, mine, MIRROR:] = later.astype(jnp.bfloat16)
+                return carry
+
+            lax.fori_loop(0, HALF, step, 0, unroll=2)
+            return carry
+
+        lax.fori_loop(0, 2, half, 0)
+        eye_row = lax.broadcasted_iota(jnp.int32, (BLK, BLK), 0)
+        eye_col = lax.broadcasted_iota(jnp.int32, (BLK, BLK), 1)
+        eye = jnp.where(eye_row == eye_col, 1.0, 0.0).astype(jnp.bfloat16)
+        for quad in range(MIRROR // 4):
+            lines = [folded[pl.ds(4 * quad + k, TILE, stride=MIRROR), :] for k in range(4)]
+            turned_over = nt_dot(eye, jnp.concatenate(lines, axis=0).astype(jnp.bfloat16))
+            mirror_out[:, quad] = turned_over.reshape(n_tm, TILE, BLK).astype(jnp.bfloat16)
+        for copy in mirror_copies():
+            copy.start()
+        mirror_in[OWN] = mirror_out[z]
+
+    def self_unfold():
+        for copy in mirror_copies():
+            copy.wait_recv()
+        place = lax.broadcasted_iota(jnp.int32, (TILE, BLK), 1) // TILE
+        sources = [opposite, down, up, z]
+        for quad in range(MIRROR // 4):
+            held = [mirror_in[slot, quad].astype(jnp.float32) for slot in range(n_tm)]
+            for k in range(4):
+                line = jnp.zeros((TILE, BLK), jnp.float32)
+                for slot, source in enumerate(sources):
+                    moved = pltpu.roll(held[slot], lax.rem(source + 4 - k, 4) * TILE, 1)
+                    line = jnp.where(place == source, moved, line)
+                unfolded[pl.ds(MIRROR - 1 - 4 * quad - k, TILE, stride=MIRROR), :] = line
+
+        def step(i, carry):
+            lines = unfolded[pl.ds(pl.multiple_of(i * MIRROR, MIRROR), MIRROR), :]
+            out_ref[0, i, :MIRROR] = lines.astype(jnp.bfloat16)
+            return carry
+
+        lax.fori_loop(0, TILE, step, 0, unroll=4)
 
     def match(p, slots):
         apart = blocks_ref[1, p] - blocks_ref[0, p]
@@ -343,6 +475,14 @@
     def kind_of(step):
         return lax.rem(step * (1 + odd), KINDS)
 
+    def self_step(tile, carry):
+        self_tile(tile)
+        return carry
+
+    zero_lag[...] = jnp.zeros_like(zero_lag)
+    lax.fori_loop(0, 4, self_step, 0)
+    self_relay()
+
     def kind_step(step, carry):
         kind = kind_of(step)
 
@@ -361,27 +501,31 @@
             to_mate().wait_recv()
 
         def tile_step(tile, carry):
-            tile_lags(step, kind, tile)
+            kind_tile(kind, tile)
             return carry
 
         lax.fori_loop(0, 4, tile_step, 0)
         relay(kind)
 
-        @pl.when(step > 0)
+        @pl.when(step == 1)
         def _():
-            finish(kind_of(step - 1))
+            self_finish()
+
+        @pl.when(step == 2)
+        def _():
+            finish(kind_of(1))
+            self_unfold()
 
         return carry
 
-    lax.fori_loop(0, KINDS, kind_step, 0)
+    lax.fori_loop(1, KINDS, kind_step, 0)
     finish(kind_of(2))
 
     to_mate().wait_send()
     forward().wait_send()
     forward().wait_recv()
-    for kind in range(KINDS):
-        for copy in sum_copies(kind):
-            copy.wait_send()
+    for copy in self_copies() + sum_copies(1) + sum_copies(2) + mirror_copies():
+        copy.wait_send()
     out_ref[3] = shared[...]
 
 
@@ -410,6 +554,8 @@
     block_len = record.shape[1]
     scale = 2.0 / math.sqrt(SEGS_DEV * n_tm * F)
     bf16 = jnp.bfloat16
+    shifts = np.arange(NLAG) - NLAG // 2
+    self_lags = lag_table(np.concatenate([np.arange(1, MIRROR + 1), np.zeros(16, np.int64)]))
     hbm = pl.BlockSpec(memory_space=pl.ANY)
     smem = pl.BlockSpec(memory_space=pltpu.SMEM)
     vmem = pl.BlockSpec(memory_space=pltpu.VMEM)
@@ -419,7 +565,7 @@
             pltpu.VMEM((4, TILE, NLAG, BLK), bf16),
             pltpu.SMEM((SLOTS,), jnp.int32),
         ),
-        in_specs=[smem, smem, smem, hbm, hbm, vmem],
+        in_specs=[smem, smem, smem, hbm, hbm, vmem, vmem],
         out_specs=(vmem, smem),
         scratch_shapes=[
             pltpu.VMEM((2 * F, SEG_LEN), bf16),
@@ -430,11 +576,21 @@
             pltpu.VMEM((KINDS, GROUPS, DEPTH, BLK), bf16),
             pltpu.VMEM((GROUPS, BLK * 8, DEPTH), bf16),
             pltpu.VMEM((TILE, 2 * F, BLK), bf16),
-            pltpu.VMEM((KINDS, 4, TILE, NLAG, BLK), bf16),
-            pltpu.VMEM((KINDS, HALF, NLAG, BLK), bf16),
-            pltpu.VMEM((KINDS, HALF, NLAG, BLK), bf16),
-            pltpu.VMEM((KINDS, TILE, NLAG, BLK), bf16),
-            pltpu.VMEM((KINDS, TILE, NLAG, BLK), bf16),
+            pltpu.VMEM((KINDS - 1, 4, TILE, NLAG, BLK), bf16),
+            pltpu.VMEM((KINDS - 1, HALF, NLAG, BLK), bf16),
+            pltpu.VMEM((KINDS - 1, HALF, NLAG, BLK), bf16),
+            pltpu.VMEM((KINDS - 1, TILE, NLAG, BLK), bf16),
+            pltpu.VMEM((KINDS - 1, TILE, NLAG, BLK), bf16),
+            pltpu.VMEM((4, 2, HALF + 1, MIRROR, BLK), bf16),
+            pltpu.VMEM((HALF + 1, MIRROR, BLK), bf16),
+            pltpu.VMEM((HALF + 1, MIRROR, BLK), bf16),
+            pltpu.VMEM((2, HALF + 1, MIRROR, BLK), bf16),
+            pltpu.VMEM((2, HALF + 1, MIRROR, BLK), bf16),
+            pltpu.VMEM((MIRROR, BLK), jnp.float32),
+            pltpu.VMEM((TILE * MIRROR, BLK), jnp.float32),
+            pltpu.VMEM((TILE * MIRROR, BLK), jnp.float32),
+            pltpu.VMEM((n_tm, MIRROR // 4, TILE, BLK), bf16),
+            pltpu.VMEM((n_tm, MIRROR // 4, TILE, BLK), bf16),
             pltpu.VMEM((TILE, NLAG, BLK), bf16),
             pltpu.SemaphoreType.DMA((block_len // 128,)),
             pltpu.SemaphoreType.DMA,
@@ -442,12 +598,14 @@
             pltpu.SemaphoreType.DMA((5,)),
             pltpu.SemaphoreType.DMA((KINDS, 6)),
             pltpu.SemaphoreType.DMA((KINDS, 6)),
+            pltpu.SemaphoreType.DMA((3,)),
+            pltpu.SemaphoreType.DMA((3,)),
         ],
         compiler_params=pltpu.CompilerParams(
             collective_id=0, has_side_effects=True, vmem_limit_bytes=60 * 1024 * 1024
         ),
         name="stacks",
-    )(seg_starts, pair_blocks.T, pair_owner, record, transform_table(), lag_table())
+    )(seg_starts, pair_blocks.T, pair_owner, record, transform_table(), lag_table(shifts), self_lags)
     return pl.pallas_call(
         place_kernel,
         out_shape=jax.ShapeDtypeStruct((TILE, SLOTS, NLAG, BLK), bf16),

time: 78.3 us -> 79 us (level)
  Pallas kernels: 77.5 us -> 78.7 us
    pallas_call x1, Pallas kernels: 76.2 us -> 77.3 us  [shards(): pl.pallas_call(functools.partial(stacks_kernel, n_chan, n_tm, scale), out...]
where the time goes in v7:
time: 79 us; the launch traced here: 78.7 us
  Pallas kernels  78.7 us (100%)
    pallas_call x1, Pallas kernels, shards(): pl.pallas_call(functools.partial(stacks_kernel, n_chan, n_tm, scale), out...  77.3 us

profile of v7, /device:TPU:1, one launch (start us, length us, event | category | flops | bytes accessed | tf_op | source)
XLA Modules:
  0.0 78.7 jit_solution(11644597103371418932)
XLA Ops:
  0.0 77.3 %stacks.1 = (bf16[4,32,64,128]{3,2,1,0:T(8,128)(2,1)S(1)}, s32[4]{0:T(128)S(4)}) custom-call(s32[16]{0:T(128)} %starts_ref.1, s32[2,93]{1,0:T(2,128)} %bitcast.1, s32[93]{0:T(128)} %owner_ref.1, bf16[128,4096]{1,0:T(8,128)(2,1)} %record_ref.1, bf16[512,512]{1,0:T(8,128)(2,1)} %constant.9.table_hbm, bf16[64,512]{1,0:T(8,128)(2,1)} %constant.10.lag_ref, ...), custom_call_target="tpu_custom_call" | custom-call | tf_op jit(solution)/shard_map/stacks/pallas_call | solution.py:562
  77.3 1.4 %place.1 = bf16[32,4,64,128]{3,2,1,0:T(8,128)(2,1)} custom-call(s32[4]{0:T(128)S(4)} %get-tuple-element.7.kinds_ref, bf16[4,32,64,128]{3,2,1,0:T(8,128)(2,1)S(1)} %get-tuple-element.8.stacks_ref), custom_call_target="tpu_custom_call" | custom-call | tf_op jit(solution)/shard_map/place/pallas_call | solution.py:609

commit v8 on v7

--- a/solution.py
+++ b/solution.py
@@ -293,7 +293,7 @@
             def _():
                 copies[index].start()
 
-    def self_tile(tile):
+    def first_gram(kind, tile):
         direct_row = lax.broadcasted_iota(jnp.int32, (8, DEPTH), 0) % 2 == 0
         row = lax.broadcasted_iota(jnp.int32, (16, DEPTH), 0)
         col = lax.broadcasted_iota(jnp.int32, (16, DEPTH), 1)
@@ -309,10 +309,19 @@
                 parts.append(jnp.concatenate(two, axis=0).astype(jnp.bfloat16) * mine)
             left = jnp.concatenate(parts, axis=0)
             expanded[group, left_rows(tile)] = left
-            cross(0, group, left)
+            cross(kind, group, left)
             return carry
 
         lax.fori_loop(0, GROUPS, expand_step, 0, unroll=4)
+
+    def later_gram(kind, tile):
+        def gram_step(group, carry):
+            cross(kind, group, expanded[group, left_rows(tile)])
+            return carry
+
+        lax.fori_loop(0, GROUPS, gram_step, 0, unroll=32)
+
+    def self_lags(tile):
         copies = self_copies()
 
         def half(h, carry):
@@ -329,12 +338,7 @@
 
         lax.fori_loop(0, 2, half, 0)
 
-    def kind_tile(kind, tile):
-        def gram_step(group, carry):
-            cross(kind, group, expanded[group, left_rows(tile)])
-            return carry
-
-        lax.fori_loop(0, GROUPS, gram_step, 0, unroll=32)
+    def kind_lags(kind, tile):
         copies = sum_copies(kind)
 
         def half(h, carry):
@@ -473,15 +477,18 @@
     transpose()
 
     def kind_of(step):
-        return lax.rem(step * (1 + odd), KINDS)
-
-    def self_step(tile, carry):
-        self_tile(tile)
-        return carry
+        return lax.rem(2 * step + 1 - odd, KINDS)
+
+    def finish_any(kind):
+        @pl.when(kind == 0)
+        def _():
+            self_finish()
+
+        @pl.when(kind > 0)
+        def _():
+            finish(kind)
 
     zero_lag[...] = jnp.zeros_like(zero_lag)
-    lax.fori_loop(0, 4, self_step, 0)
-    self_relay()
 
     def kind_step(step, carry):
         kind = kind_of(step)
@@ -501,24 +508,42 @@
             to_mate().wait_recv()
 
         def tile_step(tile, carry):
-            kind_tile(kind, tile)
+            @pl.when(step == 0)
+            def _():
+                first_gram(kind, tile)
+
+            @pl.when(step > 0)
+            def _():
+                later_gram(kind, tile)
+
+            @pl.when(kind == 0)
+            def _():
+                self_lags(tile)
+
+            @pl.when(kind > 0)
+            def _():
+                kind_lags(kind, tile)
+
             return carry
 
         lax.fori_loop(0, 4, tile_step, 0)
-        relay(kind)
-
-        @pl.when(step == 1)
-        def _():
-            self_finish()
-
-        @pl.when(step == 2)
-        def _():
-            finish(kind_of(1))
-            self_unfold()
+
+        @pl.when(kind == 0)
+        def _():
+            self_relay()
+
+        @pl.when(kind > 0)
+        def _():
+            relay(kind)
+
+        @pl.when(step > 0)
+        def _():
+            finish_any(kind_of(step - 1))
 
         return carry
 
-    lax.fori_loop(1, KINDS, kind_step, 0)
+    lax.fori_loop(0, KINDS, kind_step, 0)
+    self_unfold()
     finish(kind_of(2))
 
     to_mate().wait_send()

time: 79 us -> 77.2 us (0.977)
  Pallas kernels: 78.7 us -> 77.1 us
    pallas_call x1, Pallas kernels: 77.3 us -> 75.7 us  [shards(): pl.pallas_call(functools.partial(stacks_kernel, n_chan, n_tm, scale), out...]
where the time goes in v8:
time: 77.2 us; the launch traced here: 77.1 us
  Pallas kernels  77.1 us (100%)
    pallas_call x1, Pallas kernels, shards(): pl.pallas_call(functools.partial(stacks_kernel, n_chan, n_tm, scale), out...  75.7 us

profile of v8, /device:TPU:1, one launch (start us, length us, event | category | flops | bytes accessed | tf_op | source)
XLA Modules:
  0.0 77.1 jit_solution(5360616123623180204)
XLA Ops:
  0.0 75.7 %stacks.1 = (bf16[4,32,64,128]{3,2,1,0:T(8,128)(2,1)S(1)}, s32[4]{0:T(128)S(4)}) custom-call(s32[16]{0:T(128)} %starts_ref.1, s32[2,93]{1,0:T(2,128)} %bitcast.1, s32[93]{0:T(128)} %owner_ref.1, bf16[128,4096]{1,0:T(8,128)(2,1)} %record_ref.1, bf16[512,512]{1,0:T(8,128)(2,1)} %constant.9.table_hbm, bf16[64,512]{1,0:T(8,128)(2,1)} %constant.10.lag_ref, ...), custom_call_target="tpu_custom_call" | custom-call | tf_op jit(solution)/shard_map/stacks/pallas_call | solution.py:587
  75.7 1.4 %place.1 = bf16[32,4,64,128]{3,2,1,0:T(8,128)(2,1)} custom-call(s32[4]{0:T(128)S(4)} %get-tuple-element.7.kinds_ref, bf16[4,32,64,128]{3,2,1,0:T(8,128)(2,1)S(1)} %get-tuple-element.8.stacks_ref), custom_call_target="tpu_custom_call" | custom-call | tf_op jit(solution)/shard_map/place/pallas_call | solution.py:634

commit v9 on v8

--- a/solution.py
+++ b/solution.py
@@ -248,7 +248,7 @@
                     turned[:, rows, :] = jnp.concatenate([imag, -real], axis=1).astype(jnp.bfloat16)
             return carry
 
-        lax.fori_loop(0, SEGS_DEV // 2, step, 0, unroll=4)
+        lax.fori_loop(0, SEGS_DEV // 2, step, 0, unroll=8)
 
     def dest(tile):
         ahead = jnp.where(tile == OPP, 2, jnp.where(tile == UP, 1, jnp.where(tile == DOWN, n_tm - 1, 0)))
@@ -263,7 +263,7 @@
             sides[group] = nt_dot(eye, jnp.concatenate([spectra[0, group], turned[group]], axis=0))
             return carry
 
-        lax.fori_loop(0, GROUPS, step, 0, unroll=8)
+        lax.fori_loop(0, GROUPS, step, 0, unroll=16)
 
     def cross(kind, group, left):
         row = lax.broadcasted_iota(jnp.int32, (DEPTH, BLK), 0)
@@ -312,7 +312,7 @@
             cross(kind, group, left)
             return carry
 
-        lax.fori_loop(0, GROUPS, expand_step, 0, unroll=4)
+        lax.fori_loop(0, GROUPS, expand_step, 0, unroll=32)
 
     def later_gram(kind, tile):
         def gram_step(group, carry):

time: 77.2 us -> 77.6 us (level)
  the two profiles are of different devices: /device:TPU:1 before, /device:TPU:0 now
where the time goes in v9:
time: 77.6 us; the launch traced here: 77.4 us
  Pallas kernels  77.4 us (100%)
    pallas_call x1, Pallas kernels, shards(): pl.pallas_call(functools.partial(stacks_kernel, n_chan, n_tm, scale), out...  76 us

profile of v9, /device:TPU:0, one launch (start us, length us, event | category | flops | bytes accessed | tf_op | source)
XLA Modules:
  0.0 77.4 jit_solution(8169191762595715543)
XLA Ops:
  0.0 76.0 %stacks.1 = (bf16[4,32,64,128]{3,2,1,0:T(8,128)(2,1)S(1)}, s32[4]{0:T(128)S(4)}) custom-call(s32[16]{0:T(128)} %starts_ref.1, s32[2,93]{1,0:T(2,128)} %bitcast.1, s32[93]{0:T(128)} %owner_ref.1, bf16[128,4096]{1,0:T(8,128)(2,1)} %record_ref.1, bf16[512,512]{1,0:T(8,128)(2,1)} %constant.9.table_hbm, bf16[64,512]{1,0:T(8,128)(2,1)} %constant.10.lag_ref, ...), custom_call_target="tpu_custom_call" | custom-call | tf_op jit(solution)/shard_map/stacks/pallas_call | solution.py:587
  76.0 1.4 %place.1 = bf16[32,4,64,128]{3,2,1,0:T(8,128)(2,1)} custom-call(s32[4]{0:T(128)S(4)} %get-tuple-element.7.kinds_ref, bf16[4,32,64,128]{3,2,1,0:T(8,128)(2,1)S(1)} %get-tuple-element.8.stacks_ref), custom_call_target="tpu_custom_call" | custom-call | tf_op jit(solution)/shard_map/place/pallas_call | solution.py:634

commit v10 on v9

--- a/solution.py
+++ b/solution.py
@@ -396,7 +396,7 @@
 
         lax.fori_loop(0, TILE, step, 0, unroll=4)
 
-        @pl.when(kind == 2)
+        @pl.when((kind == 2) & (c < n_chan - 1))
         def _():
             forward().start()
 
@@ -547,11 +547,22 @@
     finish(kind_of(2))
 
     to_mate().wait_send()
-    forward().wait_send()
-    forward().wait_recv()
+
+    @pl.when(c < n_chan - 1)
+    def _():
+        forward().wait_send()
+
     for copy in self_copies() + sum_copies(1) + sum_copies(2) + mirror_copies():
         copy.wait_send()
-    out_ref[3] = shared[...]
+
+    @pl.when(c == 0)
+    def _():
+        out_ref[3] = jnp.zeros((TILE, NLAG, BLK), jnp.bfloat16)
+
+    @pl.when(c > 0)
+    def _():
+        forward().wait_recv()
+        out_ref[3] = shared[...]
 
 
 def place_kernel(kinds_ref, stacks_ref, out_ref, zeros, sem):

time: 77.6 us -> 74 us (0.954)
  the two profiles are of different devices: /device:TPU:0 before, /device:TPU:1 now
where the time goes in v10:
time: 74 us; the launch traced here: 72.7 us
  Pallas kernels  72.7 us (98%)
    pallas_call x1, Pallas kernels, shards(): pl.pallas_call(functools.partial(stacks_kernel, n_chan, n_tm, scale), out...  71.3 us

profile of v10, /device:TPU:1, one launch (start us, length us, event | category | flops | bytes accessed | tf_op | source)
XLA Modules:
  0.0 72.7 jit_solution(4990287200779239973)
XLA Ops:
  0.0 71.3 %stacks.1 = (bf16[4,32,64,128]{3,2,1,0:T(8,128)(2,1)S(1)}, s32[4]{0:T(128)S(4)}) custom-call(s32[16]{0:T(128)} %starts_ref.1, s32[2,93]{1,0:T(2,128)} %bitcast.1, s32[93]{0:T(128)} %owner_ref.1, bf16[128,4096]{1,0:T(8,128)(2,1)} %record_ref.1, bf16[512,512]{1,0:T(8,128)(2,1)} %constant.9.table_hbm, bf16[64,512]{1,0:T(8,128)(2,1)} %constant.10.lag_ref, ...), custom_call_target="tpu_custom_call" | custom-call | tf_op jit(solution)/shard_map/stacks/pallas_call | solution.py:598
  71.4 1.4 %place.1 = bf16[32,4,64,128]{3,2,1,0:T(8,128)(2,1)} custom-call(s32[4]{0:T(128)S(4)} %get-tuple-element.7.kinds_ref, bf16[4,32,64,128]{3,2,1,0:T(8,128)(2,1)S(1)} %get-tuple-element.8.stacks_ref), custom_call_target="tpu_custom_call" | custom-call | tf_op jit(solution)/shard_map/place/pallas_call | solution.py:645
